TPU v7x, 32 devices: a whole 2x2x4 slice. The times are simulated.
32 devices in a mesh: dp: 2 (over x), seq: 16 (over z, y, core).
Axes of the slice: x: 2, y: 2, z: 4, core: 2. Of those that a mesh axis runs over, the one named last changes fastest.
Arguments:
- inputs: float32 [2, 2048, 128], P('dp', 'seq'), parts along dimension 0, may hold values from -48 to 48
- trajectory: float32 [2, 2048, 128], P('dp', 'seq'), parts along dimension 0, may hold values from -0.9 to 0.9
- initial_state: float32 [2, 128], P('dp'), parts along dimension 0, may hold values from -0.9 to 0.9
- cotangent: float32 [2, 2048, 128], P('dp', 'seq'), parts along dimension 0, may hold values from -1 to 1
- in_weight: float32 [128, 384], replicated, may hold values from -0.5 to 0.5
- recurrent_weight: float32 [128, 384], replicated, may hold values from -0.5 to 0.5
- gate_bias: float32 [384], replicated
Outputs:
- new_state: float32 [2, 2048, 128], P('dp', 'seq'), parts along dimension 0
- adjoint: float32 [2, 2048, 128], P('dp', 'seq'), parts along dimension 0
There are 2 independent parts, one for each index of `dp`. A program takes and returns all parts, laid end to end along the dimension named above; an argument that names none is the same for every part. Nothing has to cross between parts.
All inputs are finite; a program needn't handle non-finite values.
Results may differ from a plain program's by a relative error of at most 0.0003.
Values sent between devices are 32-bit elements; how exact they have to be, the bound alone decides.
A program may use at most 64 MiB of HBM per device.

v0:
```python
import jax
import jax.numpy as jnp
from jax import lax
from jax.sharding import PartitionSpec as P

BLOCK = 16


HIGHEST_PRECISION = lax.Precision.HIGHEST


def passed_along(value, axis, steps):
    count = lax.axis_size(axis)
    leading, last = (max(0, -steps), min(count, count - steps))
    return lax.ppermute(value, axis, [(source, source + steps) for source in range(leading, last)])


def prefix(part, axis, combine, identity, reverse):
    count = lax.axis_size(axis)
    place = lax.axis_index(axis)
    ahead = count - 1 - place if reverse else place
    gathered = jax.tree.map(lambda a: lax.all_gather(a, axis), part)
    state = jax.tree.map(lambda a, e: jnp.zeros_like(a) + jnp.asarray(e, a.dtype), part, identity)

    def one(turn, state):
        source = count - 1 - turn if reverse else turn
        return combine(
            state, jax.tree.map(lambda a: lax.dynamic_index_in_dim(a, source, 0, False), gathered)
        )

    return lax.fori_loop(0, ahead, one, state)


def sum_parts(tensor, hidden_width):
    return (
        tensor[..., :hidden_width]
        + tensor[..., hidden_width : 2 * hidden_width]
        + tensor[..., 2 * hidden_width :]
    )


def linearize(features, previous, in_weight, recurrent_weight, gate_bias):
    hidden_width = previous.shape[-1]
    projected = (
        jnp.dot(
            features, in_weight, precision=HIGHEST_PRECISION, preferred_element_type=jnp.float32
        )
        + gate_bias
    )
    recurrent = jnp.dot(
        previous, recurrent_weight, precision=HIGHEST_PRECISION, preferred_element_type=jnp.float32
    )
    reset_gate = jax.nn.sigmoid(projected[:, :hidden_width] + recurrent[:, :hidden_width])
    write_gate = jax.nn.sigmoid(
        projected[:, hidden_width : 2 * hidden_width]
        + recurrent[:, hidden_width : 2 * hidden_width]
    )
    cand_recurrent = recurrent[:, 2 * hidden_width :]
    candidate = jnp.tanh(projected[:, 2 * hidden_width :] + reset_gate * cand_recurrent)
    updated = previous + write_gate * (candidate - previous)
    keep_rate = 1.0 - write_gate
    slopes = write_gate * (1.0 - candidate * candidate)
    gate_terms = jnp.concatenate(
        [
            slopes * cand_recurrent * reset_gate * (1.0 - reset_gate),
            (candidate - previous) * write_gate * (1.0 - write_gate),
            slopes * reset_gate,
        ],
        axis=1,
    )
    offsets = updated - keep_rate * previous - sum_parts(gate_terms * recurrent, hidden_width)
    return (keep_rate, gate_terms, offsets)


def apply_jacobian(keep_rate, gate_terms, vector, recurrent_weight):
    hidden_width = vector.shape[-1]
    mapped = jnp.einsum("bk,kj->bj", vector, recurrent_weight, precision=HIGHEST_PRECISION)
    return keep_rate * vector + sum_parts(gate_terms * mapped, hidden_width)


def apply_transposed(keep_rate, gate_terms, vector, recurrent_weight):
    tiled = jnp.concatenate([vector, vector, vector], axis=-1)
    return keep_rate * vector + jnp.einsum(
        "bk,jk->bj", gate_terms * tiled, recurrent_weight, precision=HIGHEST_PRECISION
    )


def jacobians(keep_rate, gate_terms, weight_parts):
    hidden_width = keep_rate.shape[-1]
    coupling = gate_terms[:, :hidden_width, None] * weight_parts[0][None]
    coupling = (
        coupling + gate_terms[:, hidden_width : 2 * hidden_width, None] * weight_parts[1][None]
    )
    coupling = coupling + gate_terms[:, 2 * hidden_width :, None] * weight_parts[2][None]
    return coupling + keep_rate[:, :, None] * jnp.eye(hidden_width, dtype=jnp.float32)


def matvec(matrix, vector):
    return jnp.einsum("...ij,...j->...i", matrix, vector, precision=HIGHEST_PRECISION)


def compose(earlier, later):
    return (
        jnp.matmul(later[0], earlier[0], precision=HIGHEST_PRECISION),
        matvec(later[0], earlier[1]) + later[1],
    )


def per_device(
    inputs, trajectory, initial_state, cotangent, in_weight, recurrent_weight, gate_bias
):
    tok_rows = trajectory.shape[1]
    hidden_width = trajectory.shape[2]
    position = lax.axis_index("seq")
    boundary_row = passed_along(trajectory[:, tok_rows - 1, :], "seq", 1)
    first_row = jnp.where(position == 0, initial_state, boundary_row)
    previous = jnp.concatenate([first_row, trajectory[0, : tok_rows - 1]], axis=0)
    keep_rate, gate_terms, offsets = linearize(
        inputs[0], previous, in_weight, recurrent_weight, gate_bias
    )
    blocks = tok_rows // BLOCK
    weight_parts = jnp.transpose(recurrent_weight.reshape(hidden_width, 3, hidden_width), (1, 2, 0))

    def by_step(tensor):
        return tensor.reshape(blocks, BLOCK, tensor.shape[-1]).swapaxes(0, 1)

    keep_steps = by_step(keep_rate)
    term_steps = by_step(gate_terms)
    offset_steps = by_step(offsets)
    cotan_steps = by_step(cotangent[0])
    identity = jnp.broadcast_to(
        jnp.eye(hidden_width, dtype=jnp.float32), (blocks, hidden_width, hidden_width)
    )
    zero_rows = jnp.zeros((blocks, hidden_width), jnp.float32)

    def gather_segment(carried, step_items):
        product, forward_sum, adjoint_sum = carried
        keep_now, terms_now, offset_now, cotan_now = step_items
        forward_sum = forward_sum + matvec(product, offset_now)
        costate = cotan_now + adjoint_sum
        adjoint_sum = apply_transposed(keep_now, terms_now, costate, recurrent_weight)
        product = jnp.matmul(
            product, jacobians(keep_now, terms_now, weight_parts), precision=HIGHEST_PRECISION
        )
        return ((product, forward_sum, adjoint_sum), None)

    (composite, block_offset, block_adjoint), _ = lax.scan(
        gather_segment,
        (identity, zero_rows, zero_rows),
        (keep_steps, term_steps, offset_steps, cotan_steps),
        reverse=True,
    )
    forward_maps = lax.associative_scan(compose, (composite, block_offset), axis=0)
    reverse_maps = lax.associative_scan(
        compose, (jnp.swapaxes(composite, 1, 2)[::-1], block_adjoint[::-1]), axis=0
    )
    device_matrix = forward_maps[0][blocks - 1]
    device_offset = forward_maps[1][blocks - 1]
    device_adjoint = reverse_maps[1][blocks - 1]
    start_state = initial_state[0]
    eye_matrix = jnp.eye(hidden_width, dtype=jnp.float32)
    zero_vector = jnp.zeros((hidden_width,), jnp.float32)
    prefix_matrix, prefix_offset = prefix(
        (device_matrix, device_offset), "seq", compose, (eye_matrix, zero_vector), False
    )
    entry_state = matvec(prefix_matrix, start_state) + prefix_offset
    suffix_matrix, entry_adjoint = prefix(
        (reverse_maps[0][blocks - 1], device_adjoint),
        "seq",
        compose,
        (eye_matrix, zero_vector),
        True,
    )
    block_exit = matvec(forward_maps[0], entry_state) + forward_maps[1]
    block_entry = jnp.concatenate([entry_state[None], block_exit[: blocks - 1]], axis=0)
    reverse_out = (matvec(reverse_maps[0], entry_adjoint) + reverse_maps[1])[::-1]
    block_incoming = jnp.concatenate([reverse_out[1:], entry_adjoint[None]], axis=0)

    def forward_apply(hidden_state, step_items):
        keep_now, terms_now, offset_now = step_items
        hidden_state = (
            apply_jacobian(keep_now, terms_now, hidden_state, recurrent_weight) + offset_now
        )
        return (hidden_state, hidden_state)

    _, states = lax.scan(forward_apply, block_entry, (keep_steps, term_steps, offset_steps))

    def backward_apply(carried, step_items):
        keep_now, terms_now, cotan_now = step_items
        costate = cotan_now + carried
        carried = apply_transposed(keep_now, terms_now, costate, recurrent_weight)
        return (carried, costate)

    _, adjoint_rows = lax.scan(
        backward_apply, block_incoming, (keep_steps, term_steps, cotan_steps), reverse=True
    )
    new_state = states.swapaxes(0, 1).reshape(1, tok_rows, hidden_width)
    adjoint = adjoint_rows.swapaxes(0, 1).reshape(1, tok_rows, hidden_width)
    return (new_state, adjoint)


def solution(mesh):
    return jax.shard_map(
        per_device,
        mesh=mesh,
        in_specs=(
            P("dp", "seq", None),
            P("dp", "seq", None),
            P("dp", None),
            P("dp", "seq", None),
            P(),
            P(),
            P(),
        ),
        out_specs=(P("dp", "seq", None), P("dp", "seq", None)),
        check_vma=False,
    )
```

profile of v0, /device:TPU:29, one launch (start us, length us, event | category | flops | bytes accessed | tf_op | source)
XLA Modules:
  0.0 186.7 jit_solution(1816357953636329046)
XLA Ops:
  8.0 1.3 collective-permute-start
  9.2 0.8 slice_bitcast_fusion.7
  10.2 0.8 copy-done.7
  13.8 28.2 %while.77 = (s32[]{:T(128)}, f32[8,128,128]{1,2,0:T(8,128)S(1)}, f32[8,128]{1,0:T(8,128)S(1)}, f32[8,128]{1,0:T(8,128)S(1)}, f32[16,8,384]{2,1,0:T(8,128)S(1)}, ...) while((s32[]{:T(128)}, f32[8,128,128]{1,2,0:T(8,128)S(1)}, ...), condition=%wide.region_1.2_spmd.clone, body=%wide.region_0.1_spmd.clone.sunk | while | flops 208583680 | bytes 3678371 | solution.py:147
  14.5 0.8 convolution_bitcast_fusion.9
  16.3 0.8 convolution_bitcast_fusion.9
  18.0 0.8 convolution_bitcast_fusion.9
  21.6 0.8 convolution_bitcast_fusion.9
  23.3 0.8 convolution_bitcast_fusion.9
  25.1 0.8 convolution_bitcast_fusion.9
  28.6 0.8 convolution_bitcast_fusion.9
  50.1 0.8 slice-done
  56.4 17.4 %all-gather.1 = f32[16,1,128]{2,1,0:T(1,128)S(1)} all-gather(f32[1,1,128]{2,1,0:T(1,128)S(1)} %slice_bitcast_fusion.18), channel_id=1, replica_groups=mesh['dp'=2,'seq'=16] {'seq'}, dimensions={0}, use_global_device_ids=true | all-gather | bytes 8704 | tf_op jit(solution)/shard_map/all_gather | solution.py:22
  73.8 19.7 %all-gather = f32[16,1,128]{2,1,0:T(1,128)S(1)} all-gather(f32[1,1,128]{2,1,0:T(1,128)S(1)} %slice_bitcast_fusion.19), channel_id=1, replica_groups=mesh['dp'=2,'seq'=16] {'seq'}, dimensions={0}, use_global_device_ids=true | all-gather | bytes 8704 | tf_op jit(solution)/shard_map/all_gather | solution.py:22
  94.8 26.8 %while.76 = (s32[]{:T(128)}, f32[8,128]{1,0:T(8,128)S(1)}, f32[16,8,128]{2,1,0:T(8,128)S(1)}, f32[16,8,128]{2,1,0:T(8,128)}, f32[16,8,128]{2,1,0:T(8,128)}, /*in...) while((s32[]{:T(128)}, f32[8,128]{1,0:T(8,128)S(1)}, ...), condition=%wide.region_9.10_spmd, body=%wide.region_8.9_spmd.sunk | while | flops 4730883 | bytes 242797 | solution.py:194
  95.5 0.9 convolution_add_fusion.9
  97.2 0.9 convolution_add_fusion.9
  98.9 0.9 convolution_add_fusion.9
  100.6 0.9 convolution_add_fusion.9
  102.2 0.9 convolution_add_fusion.9
  103.9 1.0 convolution_add_fusion.9
  105.6 0.9 convolution_add_fusion.9
  107.3 0.9 convolution_add_fusion.9
  109.0 1.0 convolution_add_fusion.9
  110.7 0.9 convolution_add_fusion.9
  112.3 0.9 convolution_add_fusion.9
  114.0 0.9 convolution_add_fusion.9
  115.7 0.9 convolution_add_fusion.9
  117.4 1.0 convolution_add_fusion.9
  119.1 0.9 convolution_add_fusion.9
  120.7 0.9 convolution_add_fusion.9
  122.4 8.8 %all-gather.5.cloned.1.call-done = f32[16,128,128]{2,1,0:T(8,128)} async-done(((f32[1,128,128]{2,1,0:T(8,128)}), f32[16,128,128]{2,1,0:T(8,128)}) %all-gather.5.cloned.1.call-update) | async-done | bytes 1048592 | tf_op jit(solution)/shard_map/all_gather | solution.py:22
  131.2 32.5 %while.73 = (s32[]{:T(128)}, f32[128,128]{1,0:T(8,128)S(1)}, f32[128]{0:T(128)S(1)}, s32[]{:T(128)}, f32[16,128,128]{2,1,0:T(8,128)}, /*index=5*/f32[16,128]{1,0:T(8,128)S(1)}, s32[]{:T(128)}, s32[]{:T(128)}, s32[]{:T(128)}) while((s32[]{:T(128)}, f32[128,128]{1,0:T(8,128)S(1)}, f32[128]{0:T(128)S(1)}, s32[]{:T(128)}, ...), condition=%wide.region_3.4_spmd, body=%wide.region_2.3_spmd.sunk | while | flops 25362564 | bytes 396931 | solution.py:31
  131.2 1.0 fusion.171
  132.2 1.0 fusion.170
  133.3 1.0 fusion.171
  134.4 1.0 fusion.170
  135.5 1.0 fusion.171
  136.6 1.0 fusion.170
  137.7 1.0 fusion.171
  138.7 1.0 fusion.170
  139.8 1.0 fusion.171
  140.9 1.0 fusion.170
  142.0 1.0 fusion.171
  143.1 1.0 fusion.170
  144.2 1.0 fusion.171
  145.2 1.0 fusion.170
  146.3 1.0 fusion.171
  147.4 1.0 fusion.170
  148.5 1.0 fusion.171
  149.6 1.0 fusion.170
  150.7 1.0 fusion.171
  151.7 1.0 fusion.170
  152.8 1.0 fusion.171
  153.9 1.0 fusion.170
  155.0 1.0 fusion.171
  156.1 1.0 fusion.170
  157.2 1.0 fusion.171
  158.2 1.0 fusion.170
  159.3 1.0 fusion.171
  160.4 1.0 fusion.170
  161.5 1.0 fusion.171
  162.6 1.0 fusion.170
  164.5 14.8 %while.74 = (s32[]{:T(128)}, f32[8,128]{1,0:T(8,128)S(1)}, f32[16,8,128]{2,1,0:T(8,128)S(1)}, f32[16,8,128]{2,1,0:T(8,128)}, f32[16,8,384]{2,1,0:T(8,128)S(1)}, ...) while((s32[]{:T(128)}, f32[8,128]{1,0:T(8,128)S(1)}, f32[16,8,128]{2,1,0:T(8,128)S(1)}, ...), condition=%wide.region_5.6_spmd, body=%wide.region_4.5_spmd.sunk | while | flops 4726786 | bytes 258141 | solution.py:186
  (416 shorter events, 69.3 us)
Async XLA Ops:
  7.2 3.0 %copy-start = (f32[128,384]{1,0:T(8,128)S(1)}, f32[128,384]{1,0:T(8,128)}, u32[]{:S(2)}) copy-start(f32[128,384]{1,0:T(8,128)} %param.21) | copy-start | bytes 589828
  7.2 87.0 %all-gather.7.cloned.1.call-start = ((), (), s32[]{:S(2)}) async-start(), calls=%async_computation.1 | async-start | bytes 1114112 | tf_op jit(solution)/shard_map/all_gather | solution.py:22
  8.0 4.5 %collective-permute-start = (f32[1,128]{1,0:T(1,128)S(1)}, f32[1,128]{1,0:T(1,128)S(1)}, u32[]{:S(2)}, u32[]{:S(2)}) collective-permute-start(f32[1,128]{1,0:T(1,128)S(1)} %slice_bitcast_fusion.20), channel_id=1, source_target_pairs={{0,1},{1,2},{2,3},{3,4},{4,5},{5,6},{6,7},{7,8},{8,9},{9,10},{10,1... | collective-permute-start | bytes 1544 | tf_op jit(solution)/shard_map/ppermute | solution.py:15
  10.1 0.8 copy-start.7
  10.1 0.8 copy-start.13
  10.9 0.8 copy-start.8
  11.3 0.9 copy-start.1
  12.5 0.7 copy-start.14
  42.0 0.7 copy-start.4
  42.0 0.7 copy-start.5
  42.1 0.7 copy-start.6
  43.2 5.9 %copy-start.2 = (f32[4,128,128]{2,1,0:T(8,128)}, f32[4,128,128]{2,1,0:T(8,128)S(1)}, u32[]{:S(2)}) copy-start(f32[4,128,128]{2,1,0:T(8,128)S(1)} %fusion.50) | copy-start | bytes 786436
  43.8 5.4 %copy-start.10 = (f32[4,128]{1,0:T(4,128)}, f32[4,128]{1,0:T(4,128)S(1)}, u32[]{:S(2)}) copy-start(f32[4,128]{1,0:T(4,128)S(1)} %add.336) | copy-start | bytes 6148
  44.5 0.6 copy-start.11
  46.9 6.4 %copy-start.9 = (f32[4,128]{1,0:T(4,128)}, f32[4,128]{1,0:T(4,128)S(1)}, u32[]{:S(2)}) copy-start(f32[4,128]{1,0:T(4,128)S(1)} %add.323) | copy-start | bytes 6148
  47.6 0.6 copy-start.12
  48.5 0.6 slice-start.3
  49.3 0.7 slice-start.2
  50.1 0.8 slice-start
  52.6 0.7 slice-start.4
  52.7 78.5 %all-gather.5.cloned.1.call-start = ((), (), s32[]{:S(2)}) async-start(), calls=%async_computation | async-start | bytes 1114112 | tf_op jit(solution)/shard_map/all_gather | solution.py:22
  53.5 0.7 slice-start.1
  55.4 0.8 copy-start.3
Sparse Core Ops, SparseCore 0:
  52.8 38.2 all-gather.6
  94.3 36.8 all-gather.4
where the time goes:
time: 190 us; the launch traced here: 187 us
  matrix products  82 us (43%)
  blocking collectives  37.1 us (20%)
  other arithmetic  25.3 us (13%)
  local copies, waits for them, and re-layouts  15.6 us (8%)
  between operations  14.7 us (8%)
  waiting for transfers between devices  8.82 us (5%)
    all_gather x2, blocking collectives, prefix(): gathered = jax.tree.map(lambda a: lax.all_gather(a, axis), part)  37.1 us
    dot_general x44, matrix products, matvec(): jnp.einsum('...ij,...j->...i', matrix, vector, precision=HIGHEST_PRECISION)  28.2 us
    dynamic_update_slice x32, other arithmetic, per_device(): lax.scan(forward_apply, block_entry, (keep_steps, term_steps, offset_steps))  23.1 us
    dot_general x32, matrix products, apply_transposed(): jnp.einsum('bk,jk->bj', gate_terms * tiled, recurrent_weight, precision=H...  18.8 us
    dot_general x25, matrix products, compose(): jnp.matmul(later[0], earlier[0], precision=HIGHEST_PRECISION)  18.6 us
    dot_general x16, matrix products, gather_segment(): jnp.matmul(product, jacobians(keep_now, terms_now, weight_parts), precisi...  12.3 us
    all_gather x2, waiting for transfers between devices, prefix(): gathered = jax.tree.map(lambda a: lax.all_gather(a, axis), part)  8.79 us
    unnamed x35, local copies, waits for them, and re-layouts  4.93 us
  transfers between devices with their start and end apart: 3, of which 1 were waited for; matrix products, arithmetic and copies ran while one was open for 17% of the time, Pallas kernels for 0%

commit v1 on v0

v1 whole, which is shorter than its diff:
```python
import functools

import jax
import jax.numpy as jnp
from jax import lax
from jax.experimental import pallas as pl
from jax.experimental.pallas import tpu as pltpu
from jax.sharding import PartitionSpec as P

BLOCK = 8
GROUP_LEVELS = (1, 2)
GROUP = 4
PAD = 16

HIGHEST_PRECISION = lax.Precision.HIGHEST
NT = (((1,), (1,)), ((), ()))
NN = (((1,), (0,)), ((), ()))


def split(value):
    high = value.astype(jnp.bfloat16)
    low = (value - high.astype(jnp.float32)).astype(jnp.bfloat16)
    return high, low


def product(rows, weights):
    high, low = split(rows)
    w_high, w_low = split(weights)
    width = weights.shape[1]
    stacked = jnp.concatenate(
        [
            jnp.concatenate([w_high, w_low], axis=1),
            jnp.concatenate([w_high, jnp.zeros_like(w_low)], axis=1),
        ],
        axis=0,
    )
    out = jnp.dot(
        jnp.concatenate([high, low], axis=1), stacked, preferred_element_type=jnp.float32
    )
    return out[:, :width] + out[:, width:]


def few_rows(rows, w_high, w_low, dims):
    high, low = split(rows)
    count = rows.shape[0]
    both = lax.dot_general(
        jnp.concatenate([high, low], axis=0), w_high, dims, preferred_element_type=jnp.float32
    )
    extra = lax.dot_general(high, w_low, dims, preferred_element_type=jnp.float32)
    return both[:count] + both[count:] + extra


def row_sums(matrix):
    high, low = split(matrix)
    ones = jnp.ones((PAD, matrix.shape[1]), jnp.bfloat16)
    total = lax.dot_general(ones, high, NT, preferred_element_type=jnp.float32)
    return total + lax.dot_general(ones, low, NT, preferred_element_type=jnp.float32)


def merge(early, late):
    early_map, early_adjoint = early
    late_map, late_adjoint = late
    width = early_map.shape[1]
    merged = product(early_map, late_map[:width])
    merged = jnp.concatenate([merged[:width], merged[width:] + late_map[width:]], axis=0)
    high, low = split(early_map[:width])
    adjoint = early_adjoint + few_rows(late_adjoint, high, low, NT)
    return merged, adjoint


def go_forward(node, state):
    mapped, _ = node
    width = mapped.shape[1]
    high, low = split(mapped[:width])
    return few_rows(state, high, low, NN) + mapped[width:]


def go_back(node, costate):
    mapped, adjoint = node
    width = mapped.shape[1]
    high, low = split(mapped[:width])
    return few_rows(costate, high, low, NT) + adjoint


def kernel(
    seq_count,
    features_ref,
    path_ref,
    initial_ref,
    cotan_ref,
    in_weight_ref,
    weight_ref,
    bias_ref,
    state_out,
    adjoint_out,
    previous_ref,
    keep_ref,
    term_ref,
    offset_ref,
    map_ref,
    acc_ref,
    pair_ref,
    row_ref,
    ahead_ref,
    behind_ref,
    out_ahead_ref,
    out_behind_ref,
    row_sems,
    pair_send,
    pair_recv,
    ahead_sems,
    behind_sems,
):
    rows, width = path_ref.shape
    blocks = rows // BLOCK
    me = lax.axis_index("seq")
    groups = seq_count // GROUP
    group = me // GROUP

    def at(place):
        return {"seq": place}

    barrier = pltpu.get_barrier_semaphore()
    greeted = jnp.int32(0)
    for distance in (1, GROUP):

        @pl.when(me >= distance)
        def _():
            pl.semaphore_signal(barrier, inc=1, device_id=at(me - distance))

        @pl.when(me < seq_count - distance)
        def _():
            pl.semaphore_signal(barrier, inc=1, device_id=at(me + distance))

        greeted = greeted + jnp.where(me >= distance, 1, 0)
        greeted = greeted + jnp.where(me < seq_count - distance, 1, 0)
    sides = [(me // bit) % 2 for bit in GROUP_LEVELS]
    partners = [me + bit - 2 * bit * side for bit, side in zip(GROUP_LEVELS, sides)]
    for partner in partners[1:]:
        pl.semaphore_signal(barrier, inc=1, device_id=at(partner))
        greeted = greeted + 1
    pl.semaphore_wait(barrier, greeted)

    row_copy = pltpu.make_async_remote_copy(
        src_ref=path_ref.at[pl.ds(rows - 8, 8)],
        dst_ref=row_ref,
        send_sem=row_sems.at[0],
        recv_sem=row_sems.at[1],
        device_id=at(me + 1),
    )

    @pl.when(me < seq_count - 1)
    def _():
        row_copy.start()

    projected = (
        jnp.dot(
            features_ref[...],
            in_weight_ref[...],
            precision=HIGHEST_PRECISION,
            preferred_element_type=jnp.float32,
        )
        + bias_ref[...]
    )
    previous_ref[pl.ds(1, rows - 1), :] = path_ref[pl.ds(0, rows - 1), :]

    @pl.when(me > 0)
    def _():
        row_copy.wait_recv()
        previous_ref[pl.ds(0, 1), :] = row_ref[pl.ds(7, 1), :]

    @pl.when(me == 0)
    def _():
        previous_ref[pl.ds(0, 1), :] = initial_ref[...]

    previous = previous_ref[...]
    recurrent = jnp.dot(
        previous,
        weight_ref[...],
        precision=HIGHEST_PRECISION,
        preferred_element_type=jnp.float32,
    )
    reset_gate = jax.nn.sigmoid(projected[:, :width] + recurrent[:, :width])
    write_gate = jax.nn.sigmoid(
        projected[:, width : 2 * width] + recurrent[:, width : 2 * width]
    )
    cand_recurrent = recurrent[:, 2 * width :]
    candidate = jnp.tanh(projected[:, 2 * width :] + reset_gate * cand_recurrent)
    updated = previous + write_gate * (candidate - previous)
    keep_rate = 1.0 - write_gate
    slopes = write_gate * (1.0 - candidate * candidate)
    reset_terms = slopes * cand_recurrent * reset_gate * (1.0 - reset_gate)
    write_terms = (candidate - previous) * write_gate * (1.0 - write_gate)
    cand_terms = slopes * reset_gate
    keep_ref[...] = keep_rate
    term_ref[0] = reset_terms
    term_ref[1] = write_terms
    term_ref[2] = cand_terms
    offset_ref[...] = (
        updated
        - keep_rate * previous
        - reset_terms * recurrent[:, :width]
        - write_terms * recurrent[:, width : 2 * width]
        - cand_terms * cand_recurrent
    )

    def coupling(row):
        total = weight_ref[:, pl.ds(0, width)] * term_ref[0, pl.ds(row, 1), :]
        for part in (1, 2):
            columns = pl.ds(part * width, width)
            total = total + weight_ref[:, columns] * term_ref[part, pl.ds(row, 1), :]
        return total

    diagonal = lax.broadcasted_iota(jnp.int32, (width, width), 0) == lax.broadcasted_iota(
        jnp.int32, (width, width), 1
    )
    for block in range(blocks):
        row = block * BLOCK
        first = coupling(row) + jnp.where(diagonal, keep_ref[pl.ds(row, 1), :], 0.0)
        map_ref[block, pl.ds(0, width), :] = first
        map_ref[block, pl.ds(width, PAD), :] = jnp.broadcast_to(
            offset_ref[pl.ds(row, 1), :], (PAD, width)
        )
        acc_ref[block] = first * cotan_ref[pl.ds(row, 1), :]

    def gather_step(step, carry):
        for block in range(blocks):
            row = block * BLOCK + step
            mapped = map_ref[block]
            moved = mapped * keep_ref[pl.ds(row, 1), :] + product(mapped, coupling(row))
            map_ref[block, pl.ds(0, width), :] = moved[:width]
            map_ref[block, pl.ds(width, PAD), :] = moved[width:] + offset_ref[pl.ds(row, 1), :]
            acc_ref[block] += moved[:width] * cotan_ref[pl.ds(row, 1), :]
        return carry

    lax.fori_loop(1, BLOCK, gather_step, 0)

    levels = [[(map_ref[block], row_sums(acc_ref[block])) for block in range(blocks)]]
    while len(levels[-1]) > 1:
        nodes = levels[-1]
        levels.append([merge(nodes[i], nodes[i + 1]) for i in range(0, len(nodes), 2)])

    node = levels[-1][0]
    tall = width + PAD
    copies = []
    for level in range(len(GROUP_LEVELS)):
        side = sides[level]
        pair_ref[level, side, pl.ds(0, tall), :] = node[0]
        pair_ref[level, side, pl.ds(tall, PAD), :] = node[1]
        copy = pltpu.make_async_remote_copy(
            src_ref=pair_ref.at[level, side],
            dst_ref=pair_ref.at[level, side],
            send_sem=pair_send.at[level],
            recv_sem=pair_recv.at[level],
            device_id=at(partners[level]),
        )
        copy.start()
        copies.append(copy)
        copy.wait_recv()
        node = merge(
            *[
                (pair_ref[level, i, pl.ds(0, tall), :], pair_ref[level, i, pl.ds(tall, PAD), :])
                for i in (0, 1)
            ]
        )

    ahead_copy = pltpu.make_async_remote_copy(
        src_ref=out_ahead_ref,
        dst_ref=ahead_ref,
        send_sem=ahead_sems.at[0],
        recv_sem=ahead_sems.at[1],
        device_id=at(me + GROUP),
    )
    behind_copy = pltpu.make_async_remote_copy(
        src_ref=out_behind_ref,
        dst_ref=behind_ref,
        send_sem=behind_sems.at[0],
        recv_sem=behind_sems.at[1],
        device_id=at(me - GROUP),
    )

    def pass_forward():
        @pl.when(group == 0)
        def _():
            ahead_ref[...] = jnp.broadcast_to(initial_ref[...], ahead_ref.shape)

        @pl.when(group > 0)
        def _():
            ahead_copy.wait_recv()

        @pl.when(group < groups - 1)
        def _():
            out_ahead_ref[...] = go_forward(node, ahead_ref[...])
            ahead_copy.start()

    def pass_back():
        @pl.when(group == groups - 1)
        def _():
            behind_ref[...] = jnp.zeros_like(behind_ref)

        @pl.when(group < groups - 1)
        def _():
            behind_copy.wait_recv()

        @pl.when(group > 0)
        def _():
            out_behind_ref[...] = go_back(node, behind_ref[...])
            behind_copy.start()

    @pl.when(group < groups // 2)
    def _():
        pass_forward()
        pass_back()

    @pl.when(group >= groups // 2)
    def _():
        pass_back()
        pass_forward()

    state = ahead_ref[...]
    costate = behind_ref[...]
    for level in reversed(range(len(GROUP_LEVELS))):
        early, late = [
            (pair_ref[level, i, pl.ds(0, tall), :], pair_ref[level, i, pl.ds(tall, PAD), :])
            for i in (0, 1)
        ]
        is_late = sides[level] == 1
        state, costate = (
            jnp.where(is_late, go_forward(early, state), state),
            jnp.where(is_late, costate, go_back(late, costate)),
        )

    entries = [(state, costate)]
    for nodes in reversed(levels[:-1]):
        finer = []
        for i, (state, costate) in enumerate(entries):
            early, late = nodes[2 * i], nodes[2 * i + 1]
            finer.append((state, go_back(late, costate)))
            finer.append((go_forward(early, state), costate))
        entries = finer

    states = jnp.concatenate([entry[0][:1] for entry in entries], axis=0)
    costates = jnp.concatenate([entry[1][:1] for entry in entries], axis=0)
    weight_high, weight_low = split(weight_ref[...])

    def apply_step(step, carry):
        states, costates = carry
        now = pl.ds(step, blocks, stride=BLOCK)
        mapped = few_rows(states, weight_high, weight_low, NN)
        states = keep_ref[now, :] * states + offset_ref[now, :]
        for part in range(3):
            columns = slice(part * width, (part + 1) * width)
            states = states + term_ref[part, now, :] * mapped[:, columns]
        state_out[now, :] = states

        back = pl.ds(BLOCK - 1 - step, blocks, stride=BLOCK)
        costates = cotan_ref[back, :] + costates
        adjoint_out[back, :] = costates
        spread = jnp.concatenate(
            [term_ref[part, back, :] * costates for part in range(3)], axis=1
        )
        costates = keep_ref[back, :] * costates + few_rows(spread, weight_high, weight_low, NT)
        return states, costates

    lax.fori_loop(0, BLOCK, apply_step, (states, costates))

    @pl.when(me < seq_count - 1)
    def _():
        row_copy.wait_send()

    for copy in copies:
        copy.wait_send()

    @pl.when(group < groups - 1)
    def _():
        ahead_copy.wait_send()

    @pl.when(group > 0)
    def _():
        behind_copy.wait_send()


def per_device(
    seq_count, inputs, trajectory, initial_state, cotangent, in_weight, recurrent_weight, gate_bias
):
    rows, width = trajectory.shape[1:]
    blocks = rows // BLOCK
    out = jax.ShapeDtypeStruct((rows, width), jnp.float32)
    tall = width + PAD
    vmem = functools.partial(pltpu.VMEM, dtype=jnp.float32)
    pair_sems = pltpu.SemaphoreType.DMA((2,))
    new_state, adjoint = pl.pallas_call(
        functools.partial(kernel, seq_count),
        out_shape=(out, out),
        in_specs=[pl.BlockSpec(memory_space=pltpu.VMEM)] * 7,
        out_specs=(pl.BlockSpec(memory_space=pltpu.VMEM),) * 2,
        scratch_shapes=[
            vmem((rows, width)),
            vmem((rows, width)),
            vmem((3, rows, width)),
            vmem((rows, width)),
            vmem((blocks, tall, width)),
            vmem((blocks, width, width)),
            vmem((len(GROUP_LEVELS), 2, tall + PAD, width)),
            vmem((8, width)),
            vmem((PAD, width)),
            vmem((PAD, width)),
            vmem((PAD, width)),
            vmem((PAD, width)),
            pair_sems,
            pltpu.SemaphoreType.DMA((len(GROUP_LEVELS),)),
            pltpu.SemaphoreType.DMA((len(GROUP_LEVELS),)),
            pair_sems,
            pair_sems,
        ],
        compiler_params=pltpu.CompilerParams(
            collective_id=0, has_side_effects=True, vmem_limit_bytes=40 * 1024 * 1024
        ),
        name="newton_step",
    )(
        inputs[0],
        trajectory[0],
        initial_state,
        cotangent[0],
        in_weight,
        recurrent_weight,
        gate_bias[None],
    )
    return new_state[None], adjoint[None]


def solution(mesh):
    return jax.shard_map(
        functools.partial(per_device, mesh.shape["seq"]),
        mesh=mesh,
        in_specs=(
            P("dp", "seq", None),
            P("dp", "seq", None),
            P("dp", None),
            P("dp", "seq", None),
            P(),
            P(),
            P(),
        ),
        out_specs=(P("dp", "seq", None), P("dp", "seq", None)),
        check_vma=False,
    )
```

time: 190 us -> 38 us (0.20)
  the two profiles are of different devices: /device:TPU:29 before, /device:TPU:0 now
where the time goes in v1:
time: 38 us; the launch traced here: 37.7 us
  Pallas kernels  30.1 us (79%)
  local copies, waits for them, and re-layouts  6.96 us (18%)
  between operations  0.65 us (2%)
    pallas_call x1, Pallas kernels, per_device(): pl.pallas_call(functools.partial(kernel, seq_count), out_shape=(out, out)...  30.1 us
    unnamed x16, local copies, waits for them, and re-layouts  6.96 us

profile of v1, /device:TPU:0, one launch (start us, length us, event | category | flops | bytes accessed | tf_op | source)
XLA Modules:
  0.0 37.7 jit_solution(3639460234866513156)
XLA Ops:
  0.6 0.0 copy-start.6
  0.6 0.7 %copy-done.6 = f32[384]{0:T(512)S(1)} copy-done((f32[384]{0:T(512)S(1)}, f32[384]{0:T(512)}, u32[]{:S(2)}) %copy-start.6) | copy-done | bytes 1560
  1.3 0.0 copy-start.5
  1.3 0.7 %copy-done.5 = f32[1,128]{1,0:T(1,128)S(1)} copy-done((f32[1,128]{1,0:T(1,128)S(1)}, f32[1,128]{1,0:T(1,128)}, u32[]{:S(2)}) %copy-start.5) | copy-done | bytes 536
  2.0 0.0 copy-start
  2.0 0.9 %copy-done = f32[128,384]{1,0:T(8,128)S(1)} copy-done((f32[128,384]{1,0:T(8,128)S(1)}, f32[128,384]{1,0:T(8,128)}, u32[]{:S(2)}) %copy-start) | copy-done | bytes 196632
  2.9 0.0 copy-start.1
  2.9 0.9 %copy-done.1 = f32[128,384]{1,0:T(8,128)S(1)} copy-done((f32[128,384]{1,0:T(8,128)S(1)}, f32[128,384]{1,0:T(8,128)}, u32[]{:S(2)}) %copy-start.1) | copy-done | bytes 196632
  3.8 0.0 copy-start.2
  3.8 0.8 %copy-done.2 = f32[1,128,128]{2,1,0:T(8,128)S(1)} copy-done((f32[1,128,128]{2,1,0:T(8,128)S(1)}, f32[1,128,128]{2,1,0:T(8,128)}, u32[]{:S(2)}) %copy-start.2) | copy-done | bytes 65560
  4.7 0.0 copy-start.3
  4.7 0.8 %copy-done.3 = f32[1,128,128]{2,1,0:T(8,128)S(1)} copy-done((f32[1,128,128]{2,1,0:T(8,128)S(1)}, f32[1,128,128]{2,1,0:T(8,128)}, u32[]{:S(2)}) %copy-start.3) | copy-done | bytes 65560
  5.5 0.0 copy-start.4
  5.5 0.8 %copy-done.4 = f32[1,128,128]{2,1,0:T(8,128)S(1)} copy-done((f32[1,128,128]{2,1,0:T(8,128)S(1)}, f32[1,128,128]{2,1,0:T(8,128)}, u32[]{:S(2)}) %copy-start.4) | copy-done | bytes 65560
  6.3 30.1 %newton_step.1 = (f32[128,128]{1,0:T(8,128)S(1)}, f32[128,128]{1,0:T(8,128)S(1)}) custom-call(f32[128,128]{1,0:T(8,128)S(1)} %bitcast.5, f32[128,128]{1,0:T(8,128)S(1)} %bitcast.6, f32[1,128]{1,0:T(1,128)S(1)} %copy-done.5, f32[128,128]{1,0:T(8,128)S(1)} %bitcast.7, f32[128,384]{1,0:T(8,128)S(1)} %copy-done, f32[128,384]{1,0:T(8,128)S(1)} %copy-done.1, ...), custom_call_target="tpu_custom_call" | custom-call | tf_op jit(solution)/shard_map/newton_step/pallas_call | solution.py:392
  36.4 0.6 %copy.11 = f32[1,128,128]{2,1,0:T(8,128)} copy(f32[1,128,128]{2,1,0:T(8,128)S(1)} %bitcast.9) | data formatting | bytes 131072
  37.1 0.6 %copy.12 = f32[1,128,128]{2,1,0:T(8,128)} copy(f32[1,128,128]{2,1,0:T(8,128)S(1)} %bitcast.8) | data formatting | bytes 131072
  (1 shorter events, 0.0 us)
Async XLA Ops:
  0.6 0.7 %copy-start.6 = (f32[384]{0:T(512)S(1)}, f32[384]{0:T(512)}, u32[]{:S(2)}) copy-start(f32[384]{0:T(512)} %param.13) | copy-start | bytes 4612
  1.3 0.7 %copy-start.5 = (f32[1,128]{1,0:T(1,128)S(1)}, f32[1,128]{1,0:T(1,128)}, u32[]{:S(2)}) copy-start(f32[1,128]{1,0:T(1,128)} %initial_ref.1) | copy-start | bytes 1540
  2.0 0.9 %copy-start = (f32[128,384]{1,0:T(8,128)S(1)}, f32[128,384]{1,0:T(8,128)}, u32[]{:S(2)}) copy-start(f32[128,384]{1,0:T(8,128)} %in_weight_ref.1) | copy-start | bytes 589828
  2.9 0.9 %copy-start.1 = (f32[128,384]{1,0:T(8,128)S(1)}, f32[128,384]{1,0:T(8,128)}, u32[]{:S(2)}) copy-start(f32[128,384]{1,0:T(8,128)} %weight_ref.1) | copy-start | bytes 589828
  3.8 0.8 %copy-start.2 = (f32[1,128,128]{2,1,0:T(8,128)S(1)}, f32[1,128,128]{2,1,0:T(8,128)}, u32[]{:S(2)}) copy-start(f32[1,128,128]{2,1,0:T(8,128)} %param.7) | copy-start | bytes 196612
  4.7 0.8 %copy-start.3 = (f32[1,128,128]{2,1,0:T(8,128)S(1)}, f32[1,128,128]{2,1,0:T(8,128)}, u32[]{:S(2)}) copy-start(f32[1,128,128]{2,1,0:T(8,128)} %param.8) | copy-start | bytes 196612
  5.5 0.8 %copy-start.4 = (f32[1,128,128]{2,1,0:T(8,128)S(1)}, f32[1,128,128]{2,1,0:T(8,128)}, u32[]{:S(2)}) copy-start(f32[1,128,128]{2,1,0:T(8,128)} %param.10) | copy-start | bytes 196612

commit v2 on v1

--- a/solution.py
+++ b/solution.py
@@ -68,22 +68,33 @@
     return merged, adjoint
 
 
-def go_forward(node, state):
-    mapped, _ = node
-    width = mapped.shape[1]
-    high, low = split(mapped[:width])
-    return few_rows(state, high, low, NN) + mapped[width:]
-
-
-def go_back(node, costate):
+def in_parts(node):
     mapped, adjoint = node
     width = mapped.shape[1]
-    high, low = split(mapped[:width])
+    return (*split(mapped[:width]), mapped[width:], adjoint)
+
+
+def go_forward(parts, state):
+    high, low, offset, _ = parts
+    return few_rows(state, high, low, NN) + offset
+
+
+def go_back(parts, costate):
+    high, low, _, adjoint = parts
     return few_rows(costate, high, low, NT) + adjoint
 
 
 def kernel(
     seq_count,
+    features_hbm,
+    path_hbm,
+    initial_hbm,
+    cotan_hbm,
+    in_weight_hbm,
+    weight_hbm,
+    bias_hbm,
+    state_out,
+    adjoint_out,
     features_ref,
     path_ref,
     initial_ref,
@@ -91,8 +102,7 @@
     in_weight_ref,
     weight_ref,
     bias_ref,
-    state_out,
-    adjoint_out,
+    fetch_sems,
     previous_ref,
     keep_ref,
     term_ref,
@@ -111,7 +121,7 @@
     ahead_sems,
     behind_sems,
 ):
-    rows, width = path_ref.shape
+    rows, width = path_hbm.shape
     blocks = rows // BLOCK
     me = lax.axis_index("seq")
     groups = seq_count // GROUP
@@ -119,6 +129,20 @@
 
     def at(place):
         return {"seq": place}
+
+    fetches = []
+    for source, target in (
+        (path_hbm, path_ref),
+        (features_hbm, features_ref),
+        (in_weight_hbm, in_weight_ref),
+        (bias_hbm, bias_ref),
+        (weight_hbm, weight_ref),
+        (initial_hbm, initial_ref),
+        (cotan_hbm, cotan_ref),
+    ):
+        fetch = pltpu.make_async_copy(source, target, fetch_sems.at[len(fetches)])
+        fetch.start()
+        fetches.append(fetch)
 
     barrier = pltpu.get_barrier_semaphore()
     greeted = jnp.int32(0)
@@ -142,7 +166,7 @@
     pl.semaphore_wait(barrier, greeted)
 
     row_copy = pltpu.make_async_remote_copy(
-        src_ref=path_ref.at[pl.ds(rows - 8, 8)],
+        src_ref=path_hbm.at[pl.ds(rows - 8, 8)],
         dst_ref=row_ref,
         send_sem=row_sems.at[0],
         recv_sem=row_sems.at[1],
@@ -152,6 +176,9 @@
     @pl.when(me < seq_count - 1)
     def _():
         row_copy.start()
+
+    for fetch in fetches[:4]:
+        fetch.wait()
 
     projected = (
         jnp.dot(
@@ -160,9 +187,12 @@
             precision=HIGHEST_PRECISION,
             preferred_element_type=jnp.float32,
         )
-        + bias_ref[...]
+        + bias_ref[...][None, :]
     )
     previous_ref[pl.ds(1, rows - 1), :] = path_ref[pl.ds(0, rows - 1), :]
+
+    for fetch in fetches[4:]:
+        fetch.wait()
 
     @pl.when(me > 0)
     def _():
@@ -243,6 +273,7 @@
     node = levels[-1][0]
     tall = width + PAD
     copies = []
+    pair_parts = []
     for level in range(len(GROUP_LEVELS)):
         side = sides[level]
         pair_ref[level, side, pl.ds(0, tall), :] = node[0]
@@ -257,13 +288,14 @@
         copy.start()
         copies.append(copy)
         copy.wait_recv()
-        node = merge(
-            *[
-                (pair_ref[level, i, pl.ds(0, tall), :], pair_ref[level, i, pl.ds(tall, PAD), :])
-                for i in (0, 1)
-            ]
-        )
-
+        pair = [
+            (pair_ref[level, i, pl.ds(0, tall), :], pair_ref[level, i, pl.ds(tall, PAD), :])
+            for i in (0, 1)
+        ]
+        pair_parts.append([in_parts(one) for one in pair])
+        node = merge(*pair)
+
+    whole = in_parts(node)
     ahead_copy = pltpu.make_async_remote_copy(
         src_ref=out_ahead_ref,
         dst_ref=ahead_ref,
@@ -290,7 +322,7 @@
 
         @pl.when(group < groups - 1)
         def _():
-            out_ahead_ref[...] = go_forward(node, ahead_ref[...])
+            out_ahead_ref[...] = go_forward(whole, ahead_ref[...])
             ahead_copy.start()
 
     def pass_back():
@@ -304,7 +336,7 @@
 
         @pl.when(group > 0)
         def _():
-            out_behind_ref[...] = go_back(node, behind_ref[...])
+            out_behind_ref[...] = go_back(whole, behind_ref[...])
             behind_copy.start()
 
     @pl.when(group < groups // 2)
@@ -320,10 +352,7 @@
     state = ahead_ref[...]
     costate = behind_ref[...]
     for level in reversed(range(len(GROUP_LEVELS))):
-        early, late = [
-            (pair_ref[level, i, pl.ds(0, tall), :], pair_ref[level, i, pl.ds(tall, PAD), :])
-            for i in (0, 1)
-        ]
+        early, late = pair_parts[level]
         is_late = sides[level] == 1
         state, costate = (
             jnp.where(is_late, go_forward(early, state), state),
@@ -334,7 +363,7 @@
     for nodes in reversed(levels[:-1]):
         finer = []
         for i, (state, costate) in enumerate(entries):
-            early, late = nodes[2 * i], nodes[2 * i + 1]
+            early, late = in_parts(nodes[2 * i]), in_parts(nodes[2 * i + 1])
             finer.append((state, go_back(late, costate)))
             finer.append((go_forward(early, state), costate))
         entries = finer
@@ -392,9 +421,17 @@
     new_state, adjoint = pl.pallas_call(
         functools.partial(kernel, seq_count),
         out_shape=(out, out),
-        in_specs=[pl.BlockSpec(memory_space=pltpu.VMEM)] * 7,
+        in_specs=[pl.BlockSpec(memory_space=pltpu.HBM)] * 7,
         out_specs=(pl.BlockSpec(memory_space=pltpu.VMEM),) * 2,
         scratch_shapes=[
+            vmem(inputs.shape[1:]),
+            vmem((rows, width)),
+            vmem((1, width)),
+            vmem((rows, width)),
+            vmem(in_weight.shape),
+            vmem(recurrent_weight.shape),
+            vmem((3 * width,)),
+            pltpu.SemaphoreType.DMA((7,)),
             vmem((rows, width)),
             vmem((rows, width)),
             vmem((3, rows, width)),
@@ -414,7 +451,7 @@
             pair_sems,
         ],
         compiler_params=pltpu.CompilerParams(
-            collective_id=0, has_side_effects=True, vmem_limit_bytes=40 * 1024 * 1024
+            collective_id=0, has_side_effects=True, vmem_limit_bytes=64 * 1024 * 1024
         ),
         name="newton_step",
     )(
@@ -424,7 +461,7 @@
         cotangent[0],
         in_weight,
         recurrent_weight,
-        gate_bias[None],
+        gate_bias,
     )
     return new_state[None], adjoint[None]
 

time: 38 us -> 33.9 us (0.89)
  local copies, waits for them, and re-layouts: 6.96 us -> 2.14 us
  Pallas kernels: 30.1 us -> 31 us
    unnamed x16 -> x4, local copies, waits for them, and re-layouts: 6.96 us -> 2.14 us
    pallas_call x1, Pallas kernels: 30.1 us -> 31 us  [per_device(): pl.pallas_call(functools.partial(kernel, seq_count), out_shape=(out, out)...]
where the time goes in v2:
time: 33.9 us; the launch traced here: 33.7 us
  Pallas kernels  31 us (91%)
  local copies, waits for them, and re-layouts  2.14 us (6%)
  between operations  0.65 us (2%)
    pallas_call x1, Pallas kernels, per_device(): pl.pallas_call(functools.partial(kernel, seq_count), out_shape=(out, out)...  31 us
    unnamed x4, local copies, waits for them, and re-layouts  2.14 us

profile of v2, /device:TPU:0, one launch (start us, length us, event | category | flops | bytes accessed | tf_op | source)
XLA Modules:
  0.0 33.7 jit_solution(7023200735153997205)
XLA Ops:
  0.6 31.0 %newton_step.1 = (f32[128,128]{1,0:T(8,128)}, f32[128,128]{1,0:T(8,128)}) custom-call(f32[128,128]{1,0:T(8,128)} %bitcast.7, f32[128,128]{1,0:T(8,128)} %bitcast.8, f32[1,128]{1,0:T(1,128)} %initial_hbm.1, f32[128,128]{1,0:T(8,128)} %bitcast.9, f32[128,384]{1,0:T(8,128)} %in_weight_hbm.1, f32[128,384]{1,0:T(8,128)} %weight_hbm.1, f32[384]{0:T(512)} %bias_hbm.1), custom_call_target="tpu_custom_call" | custom-call | tf_op jit(solution)/shard_map/newton_step/pallas_call | solution.py:421
  31.6 0.0 copy-start
  31.6 1.5 %copy.11 = f32[1,128,128]{2,1,0:T(8,128)} copy(f32[1,128,128]{2,1,0:T(8,128)} %bitcast.6) | data formatting | bytes 131072
  33.1 0.0 copy-done
  33.1 0.6 %copy.12 = f32[1,128,128]{2,1,0:T(8,128)} copy(f32[1,128,128]{2,1,0:T(8,128)S(1)} %bitcast.5) | data formatting | bytes 131072
Async XLA Ops:
  31.6 1.5 %copy-start = (f32[128,128]{1,0:T(8,128)S(1)}, f32[128,128]{1,0:T(8,128)}, u32[]{:S(2)}) copy-start(f32[128,128]{1,0:T(8,128)} %get-tuple-element.5) | copy-start | bytes 196612

commit v3 on v2

--- a/solution.py
+++ b/solution.py
@@ -12,7 +12,6 @@
 GROUP = 4
 PAD = 16
 
-HIGHEST_PRECISION = lax.Precision.HIGHEST
 NT = (((1,), (1,)), ((), ()))
 NN = (((1,), (0,)), ((), ()))
 
@@ -23,10 +22,9 @@
     return high, low
 
 
-def product(rows, weights):
-    high, low = split(rows)
-    w_high, w_low = split(weights)
-    width = weights.shape[1]
+def product_of_parts(rows, weights):
+    (high, low), (w_high, w_low) = rows, weights
+    width = w_high.shape[1]
     stacked = jnp.concatenate(
         [
             jnp.concatenate([w_high, w_low], axis=1),
@@ -40,48 +38,55 @@
     return out[:, :width] + out[:, width:]
 
 
-def few_rows(rows, w_high, w_low, dims):
-    high, low = split(rows)
+def product(rows, weights):
+    return product_of_parts(split(rows), split(weights))
+
+
+def few_rows(rows, parts, dims):
     count = rows.shape[0]
-    both = lax.dot_general(
-        jnp.concatenate([high, low], axis=0), w_high, dims, preferred_element_type=jnp.float32
-    )
-    extra = lax.dot_general(high, w_low, dims, preferred_element_type=jnp.float32)
-    return both[:count] + both[count:] + extra
+    side = 1 - dims[0][1][0]
+    width = parts[0].shape[side]
+    out = lax.dot_general(
+        jnp.concatenate(split(rows), axis=0),
+        jnp.concatenate(parts, axis=side),
+        dims,
+        preferred_element_type=jnp.float32,
+    )
+    return out[:count, :width] + out[count:, :width] + out[:count, width:]
 
 
 def row_sums(matrix):
-    high, low = split(matrix)
-    ones = jnp.ones((PAD, matrix.shape[1]), jnp.bfloat16)
-    total = lax.dot_general(ones, high, NT, preferred_element_type=jnp.float32)
-    return total + lax.dot_general(ones, low, NT, preferred_element_type=jnp.float32)
+    ones = jnp.ones((PAD, 2 * matrix.shape[1]), jnp.bfloat16)
+    return lax.dot_general(
+        ones,
+        jnp.concatenate(split(matrix), axis=1),
+        NT,
+        preferred_element_type=jnp.float32,
+    )
+
+
+def node_of(mapped, adjoint):
+    return mapped, split(mapped), adjoint
+
+
+def matrix_parts(node):
+    width = node[0].shape[1]
+    return tuple(part[:width] for part in node[1])
 
 
 def merge(early, late):
-    early_map, early_adjoint = early
-    late_map, late_adjoint = late
-    width = early_map.shape[1]
-    merged = product(early_map, late_map[:width])
-    merged = jnp.concatenate([merged[:width], merged[width:] + late_map[width:]], axis=0)
-    high, low = split(early_map[:width])
-    adjoint = early_adjoint + few_rows(late_adjoint, high, low, NT)
-    return merged, adjoint
-
-
-def in_parts(node):
-    mapped, adjoint = node
-    width = mapped.shape[1]
-    return (*split(mapped[:width]), mapped[width:], adjoint)
-
-
-def go_forward(parts, state):
-    high, low, offset, _ = parts
-    return few_rows(state, high, low, NN) + offset
-
-
-def go_back(parts, costate):
-    high, low, _, adjoint = parts
-    return few_rows(costate, high, low, NT) + adjoint
+    width = early[0].shape[1]
+    merged = product_of_parts(early[1], matrix_parts(late))
+    merged = jnp.concatenate([merged[:width], merged[width:] + late[0][width:]], axis=0)
+    return node_of(merged, early[2] + few_rows(late[2], matrix_parts(early), NT))
+
+
+def go_forward(node, state):
+    return few_rows(state, matrix_parts(node), NN) + node[0][state.shape[1] :]
+
+
+def go_back(node, costate):
+    return few_rows(costate, matrix_parts(node), NT) + node[2]
 
 
 def kernel(
@@ -181,12 +186,7 @@
         fetch.wait()
 
     projected = (
-        jnp.dot(
-            features_ref[...],
-            in_weight_ref[...],
-            precision=HIGHEST_PRECISION,
-            preferred_element_type=jnp.float32,
-        )
+        product(features_ref[...], in_weight_ref[...])
         + bias_ref[...][None, :]
     )
     previous_ref[pl.ds(1, rows - 1), :] = path_ref[pl.ds(0, rows - 1), :]
@@ -204,12 +204,8 @@
         previous_ref[pl.ds(0, 1), :] = initial_ref[...]
 
     previous = previous_ref[...]
-    recurrent = jnp.dot(
-        previous,
-        weight_ref[...],
-        precision=HIGHEST_PRECISION,
-        preferred_element_type=jnp.float32,
-    )
+    weight_parts = split(weight_ref[...])
+    recurrent = product_of_parts(split(previous), weight_parts)
     reset_gate = jax.nn.sigmoid(projected[:, :width] + recurrent[:, :width])
     write_gate = jax.nn.sigmoid(
         projected[:, width : 2 * width] + recurrent[:, width : 2 * width]
@@ -265,7 +261,7 @@
 
     lax.fori_loop(1, BLOCK, gather_step, 0)
 
-    levels = [[(map_ref[block], row_sums(acc_ref[block])) for block in range(blocks)]]
+    levels = [[node_of(map_ref[block], row_sums(acc_ref[block])) for block in range(blocks)]]
     while len(levels[-1]) > 1:
         nodes = levels[-1]
         levels.append([merge(nodes[i], nodes[i + 1]) for i in range(0, len(nodes), 2)])
@@ -273,11 +269,11 @@
     node = levels[-1][0]
     tall = width + PAD
     copies = []
-    pair_parts = []
+    pairs = []
     for level in range(len(GROUP_LEVELS)):
         side = sides[level]
         pair_ref[level, side, pl.ds(0, tall), :] = node[0]
-        pair_ref[level, side, pl.ds(tall, PAD), :] = node[1]
+        pair_ref[level, side, pl.ds(tall, PAD), :] = node[2]
         copy = pltpu.make_async_remote_copy(
             src_ref=pair_ref.at[level, side],
             dst_ref=pair_ref.at[level, side],
@@ -289,13 +285,12 @@
         copies.append(copy)
         copy.wait_recv()
         pair = [
-            (pair_ref[level, i, pl.ds(0, tall), :], pair_ref[level, i, pl.ds(tall, PAD), :])
+            node_of(pair_ref[level, i, pl.ds(0, tall), :], pair_ref[level, i, pl.ds(tall, PAD), :])
             for i in (0, 1)
         ]
-        pair_parts.append([in_parts(one) for one in pair])
+        pairs.append(pair)
         node = merge(*pair)
 
-    whole = in_parts(node)
     ahead_copy = pltpu.make_async_remote_copy(
         src_ref=out_ahead_ref,
         dst_ref=ahead_ref,
@@ -322,7 +317,7 @@
 
         @pl.when(group < groups - 1)
         def _():
-            out_ahead_ref[...] = go_forward(whole, ahead_ref[...])
+            out_ahead_ref[...] = go_forward(node, ahead_ref[...])
             ahead_copy.start()
 
     def pass_back():
@@ -336,7 +331,7 @@
 
         @pl.when(group > 0)
         def _():
-            out_behind_ref[...] = go_back(whole, behind_ref[...])
+            out_behind_ref[...] = go_back(node, behind_ref[...])
             behind_copy.start()
 
     @pl.when(group < groups // 2)
@@ -352,7 +347,7 @@
     state = ahead_ref[...]
     costate = behind_ref[...]
     for level in reversed(range(len(GROUP_LEVELS))):
-        early, late = pair_parts[level]
+        early, late = pairs[level]
         is_late = sides[level] == 1
         state, costate = (
             jnp.where(is_late, go_forward(early, state), state),
@@ -363,19 +358,18 @@
     for nodes in reversed(levels[:-1]):
         finer = []
         for i, (state, costate) in enumerate(entries):
-            early, late = in_parts(nodes[2 * i]), in_parts(nodes[2 * i + 1])
+            early, late = nodes[2 * i], nodes[2 * i + 1]
             finer.append((state, go_back(late, costate)))
             finer.append((go_forward(early, state), costate))
         entries = finer
 
     states = jnp.concatenate([entry[0][:1] for entry in entries], axis=0)
     costates = jnp.concatenate([entry[1][:1] for entry in entries], axis=0)
-    weight_high, weight_low = split(weight_ref[...])
 
     def apply_step(step, carry):
         states, costates = carry
         now = pl.ds(step, blocks, stride=BLOCK)
-        mapped = few_rows(states, weight_high, weight_low, NN)
+        mapped = few_rows(states, weight_parts, NN)
         states = keep_ref[now, :] * states + offset_ref[now, :]
         for part in range(3):
             columns = slice(part * width, (part + 1) * width)
@@ -388,7 +382,7 @@
         spread = jnp.concatenate(
             [term_ref[part, back, :] * costates for part in range(3)], axis=1
         )
-        costates = keep_ref[back, :] * costates + few_rows(spread, weight_high, weight_low, NT)
+        costates = keep_ref[back, :] * costates + few_rows(spread, weight_parts, NT)
         return states, costates
 
     lax.fori_loop(0, BLOCK, apply_step, (states, costates))

time: 33.9 us -> 33.1 us (0.976)
  Pallas kernels: 31 us -> 30.1 us
    pallas_call x1, Pallas kernels: 31 us -> 30.1 us  [per_device(): pl.pallas_call(functools.partial(kernel, seq_count), out_shape=(out, out)...]
where the time goes in v3:
time: 33.1 us; the launch traced here: 32.9 us
  Pallas kernels  30.1 us (91%)
  local copies, waits for them, and re-layouts  2.14 us (6%)
  between operations  0.65 us (2%)
    pallas_call x1, Pallas kernels, per_device(): pl.pallas_call(functools.partial(kernel, seq_count), out_shape=(out, out)...  30.1 us
    unnamed x4, local copies, waits for them, and re-layouts  2.14 us

profile of v3, /device:TPU:0, one launch (start us, length us, event | category | flops | bytes accessed | tf_op | source)
XLA Modules:
  0.0 32.9 jit_solution(13371962646090423682)
XLA Ops:
  0.6 30.1 %newton_step.1 = (f32[128,128]{1,0:T(8,128)}, f32[128,128]{1,0:T(8,128)}) custom-call(f32[128,128]{1,0:T(8,128)} %bitcast.7, f32[128,128]{1,0:T(8,128)} %bitcast.8, f32[1,128]{1,0:T(1,128)} %initial_hbm.1, f32[128,128]{1,0:T(8,128)} %bitcast.9, f32[128,384]{1,0:T(8,128)} %in_weight_hbm.1, f32[128,384]{1,0:T(8,128)} %weight_hbm.1, f32[384]{0:T(512)} %bias_hbm.1), custom_call_target="tpu_custom_call" | custom-call | tf_op jit(solution)/shard_map/newton_step/pallas_call | solution.py:415
  30.8 0.0 copy-start
  30.8 1.5 %copy.11 = f32[1,128,128]{2,1,0:T(8,128)} copy(f32[1,128,128]{2,1,0:T(8,128)} %bitcast.6) | data formatting | bytes 131072
  32.3 0.0 copy-done
  32.3 0.6 %copy.12 = f32[1,128,128]{2,1,0:T(8,128)} copy(f32[1,128,128]{2,1,0:T(8,128)S(1)} %bitcast.5) | data formatting | bytes 131072
Async XLA Ops:
  30.8 1.5 %copy-start = (f32[128,128]{1,0:T(8,128)S(1)}, f32[128,128]{1,0:T(8,128)}, u32[]{:S(2)}) copy-start(f32[128,128]{1,0:T(8,128)} %get-tuple-element.5) | copy-start | bytes 196612

commit v4 on v3

--- a/solution.py
+++ b/solution.py
@@ -401,6 +401,19 @@
     @pl.when(group > 0)
     def _():
         behind_copy.wait_send()
+
+
+def hand_over_kernel(state_in, adjoint_in, state_out, adjoint_out, sems):
+    copies = [
+        pltpu.make_async_copy(source, target, sems.at[index])
+        for index, (source, target) in enumerate(
+            ((state_in, state_out), (adjoint_in, adjoint_out))
+        )
+    ]
+    for copy in copies:
+        copy.start()
+    for copy in copies:
+        copy.wait()
 
 
 def per_device(
@@ -457,6 +470,15 @@
         recurrent_weight,
         gate_bias,
     )
+    new_state, adjoint = pl.pallas_call(
+        hand_over_kernel,
+        out_shape=(out, out),
+        in_specs=[pl.BlockSpec(memory_space=pl.ANY)] * 2,
+        out_specs=(pl.BlockSpec(memory_space=pl.ANY),) * 2,
+        scratch_shapes=[pltpu.SemaphoreType.DMA((2,))],
+        compiler_params=pltpu.CompilerParams(vmem_limit_bytes=64 * 1024 * 1024),
+        name="hand_over",
+    )(new_state, adjoint)
     return new_state[None], adjoint[None]
 
 

time: 33.1 us -> 36 us (1.088)
  Pallas kernels: 30.1 us -> 35.2 us
  local copies, waits for them, and re-layouts: 2.14 us -> 0 us
    pallas_call x0 -> x1, Pallas kernels: none -> 5.09 us  [per_device(): pl.pallas_call(hand_over_kernel, out_shape=(out, out), in_specs=[pl.Block...]
    unnamed x4 -> x0, local copies, waits for them, and re-layouts: 2.14 us -> none
where the time goes in v4:
time: 36 us; the launch traced here: 35.8 us
  Pallas kernels  35.2 us (98%)
  between operations  0.64 us (2%)
    pallas_call x1, Pallas kernels, per_device(): pl.pallas_call(functools.partial(kernel, seq_count), out_shape=(out, out)...  30.1 us
    pallas_call x1, Pallas kernels, per_device(): pl.pallas_call(hand_over_kernel, out_shape=(out, out), in_specs=[pl.Block...  5.09 us

profile of v4, /device:TPU:0, one launch (start us, length us, event | category | flops | bytes accessed | tf_op | source)
XLA Modules:
  0.0 35.8 jit_solution(3768386255183790396)
XLA Ops:
  0.6 30.1 %newton_step.1 = (f32[128,128]{1,0:T(8,128)}, f32[128,128]{1,0:T(8,128)}) custom-call(f32[128,128]{1,0:T(8,128)} %bitcast.5, f32[128,128]{1,0:T(8,128)} %bitcast.6, f32[1,128]{1,0:T(1,128)} %initial_hbm.1, f32[128,128]{1,0:T(8,128)} %bitcast.7, f32[128,384]{1,0:T(8,128)} %in_weight_hbm.1, f32[128,384]{1,0:T(8,128)} %weight_hbm.1, f32[384]{0:T(512)} %bias_hbm.1), custom_call_target="tpu_custom_call" | custom-call | tf_op jit(solution)/shard_map/newton_step/pallas_call | solution.py:428
  30.8 5.1 %hand_over.1 = (f32[128,128]{1,0:T(8,128)}, f32[128,128]{1,0:T(8,128)}) custom-call(f32[128,128]{1,0:T(8,128)} %get-tuple-element.6.state_in, f32[128,128]{1,0:T(8,128)} %get-tuple-element.7.adjoint_in), custom_call_target="tpu_custom_call" | custom-call | tf_op jit(solution)/shard_map/hand_over/pallas_call | solution.py:473

commit v5 on v3

--- a/solution.py
+++ b/solution.py
@@ -11,6 +11,7 @@
 GROUP_LEVELS = (1, 2)
 GROUP = 4
 PAD = 16
+SENT = 8
 
 NT = (((1,), (1,)), ((), ()))
 NN = (((1,), (0,)), ((), ()))
@@ -267,29 +268,48 @@
         levels.append([merge(nodes[i], nodes[i + 1]) for i in range(0, len(nodes), 2)])
 
     node = levels[-1][0]
-    tall = width + PAD
-    copies = []
-    pairs = []
-    for level in range(len(GROUP_LEVELS)):
-        side = sides[level]
-        pair_ref[level, side, pl.ds(0, tall), :] = node[0]
-        pair_ref[level, side, pl.ds(tall, PAD), :] = node[2]
+    tall = width + 2 * SENT
+    half = tall // 2
+
+    def write_message(target, node):
+        target[pl.ds(0, width + SENT), :] = node[0][: width + SENT]
+        target[pl.ds(width + SENT, SENT), :] = node[2][:SENT]
+
+    def read_message(source):
+        offset = source[pl.ds(width, SENT), :]
+        adjoint = source[pl.ds(width + SENT, SENT), :]
+        return node_of(
+            jnp.concatenate([source[pl.ds(0, width), :], offset, offset], axis=0),
+            jnp.concatenate([adjoint, adjoint], axis=0),
+        )
+
+    def send(ref, index, partner):
         copy = pltpu.make_async_remote_copy(
-            src_ref=pair_ref.at[level, side],
-            dst_ref=pair_ref.at[level, side],
-            send_sem=pair_send.at[level],
-            recv_sem=pair_recv.at[level],
-            device_id=at(partners[level]),
+            src_ref=ref,
+            dst_ref=ref,
+            send_sem=pair_send.at[index],
+            recv_sem=pair_recv.at[index],
+            device_id=at(partner),
         )
         copy.start()
-        copies.append(copy)
-        copy.wait_recv()
-        pair = [
-            node_of(pair_ref[level, i, pl.ds(0, tall), :], pair_ref[level, i, pl.ds(tall, PAD), :])
-            for i in (0, 1)
-        ]
-        pairs.append(pair)
-        node = merge(*pair)
+        return copy
+
+    pairs = []
+    write_message(pair_ref.at[0, sides[0]], node)
+    sibling_copy = send(pair_ref.at[0, sides[0]], 0, partners[0])
+    sibling_copy.wait_recv()
+    pairs.append([read_message(pair_ref.at[0, i]) for i in (0, 1)])
+    node = merge(*pairs[0])
+
+    write_message(pair_ref.at[1, sides[1]], node)
+    my_half = pl.ds(pl.multiple_of(half * sides[0], SENT), half)
+    half_copy = send(pair_ref.at[1, sides[1], my_half], 1, partners[1])
+    half_copy.wait_recv()
+    shared_copy = send(pair_ref.at[1, 1 - sides[1], my_half], 2, partners[0])
+    shared_copy.wait_recv()
+    pairs.append([read_message(pair_ref.at[1, i]) for i in (0, 1)])
+    node = merge(*pairs[1])
+    copies = [sibling_copy, half_copy, shared_copy]
 
     ahead_copy = pltpu.make_async_remote_copy(
         src_ref=out_ahead_ref,
@@ -306,6 +326,9 @@
         device_id=at(me - GROUP),
     )
 
+    def doubled(ref):
+        return jnp.concatenate([ref[...], ref[...]], axis=0)
+
     def pass_forward():
         @pl.when(group == 0)
         def _():
@@ -317,21 +340,23 @@
 
         @pl.when(group < groups - 1)
         def _():
-            out_ahead_ref[...] = go_forward(node, ahead_ref[...])
+            out_ahead_ref[...] = go_forward(node, doubled(ahead_ref))[:SENT]
             ahead_copy.start()
 
     def pass_back():
         @pl.when(group == groups - 1)
         def _():
             behind_ref[...] = jnp.zeros_like(behind_ref)
+            out_behind_ref[...] = node[2][:SENT]
 
         @pl.when(group < groups - 1)
         def _():
             behind_copy.wait_recv()
 
+            out_behind_ref[...] = go_back(node, doubled(behind_ref))[:SENT]
+
         @pl.when(group > 0)
         def _():
-            out_behind_ref[...] = go_back(node, behind_ref[...])
             behind_copy.start()
 
     @pl.when(group < groups // 2)
@@ -344,8 +369,8 @@
         pass_back()
         pass_forward()
 
-    state = ahead_ref[...]
-    costate = behind_ref[...]
+    state = doubled(ahead_ref)
+    costate = doubled(behind_ref)
     for level in reversed(range(len(GROUP_LEVELS))):
         early, late = pairs[level]
         is_late = sides[level] == 1
@@ -432,15 +457,15 @@
             vmem((rows, width)),
             vmem((blocks, tall, width)),
             vmem((blocks, width, width)),
-            vmem((len(GROUP_LEVELS), 2, tall + PAD, width)),
+            vmem((len(GROUP_LEVELS), 2, width + 2 * SENT, width)),
             vmem((8, width)),
-            vmem((PAD, width)),
-            vmem((PAD, width)),
-            vmem((PAD, width)),
-            vmem((PAD, width)),
+            vmem((SENT, width)),
+            vmem((SENT, width)),
+            vmem((SENT, width)),
+            vmem((SENT, width)),
             pair_sems,
-            pltpu.SemaphoreType.DMA((len(GROUP_LEVELS),)),
-            pltpu.SemaphoreType.DMA((len(GROUP_LEVELS),)),
+            pltpu.SemaphoreType.DMA((3,)),
+            pltpu.SemaphoreType.DMA((3,)),
             pair_sems,
             pair_sems,
         ],

time: 33.1 us -> 33.2 us (level)
  no operation moved by 1% of the time
where the time goes in v5:
time: 33.2 us; the launch traced here: 33.1 us
  Pallas kernels  30.3 us (91%)
  local copies, waits for them, and re-layouts  2.14 us (6%)
  between operations  0.65 us (2%)
    pallas_call x1, Pallas kernels, per_device(): pl.pallas_call(functools.partial(kernel, seq_count), out_shape=(out, out)...  30.3 us
    unnamed x4, local copies, waits for them, and re-layouts  2.14 us

profile of v5, /device:TPU:0, one launch (start us, length us, event | category | flops | bytes accessed | tf_op | source)
XLA Modules:
  0.0 33.1 jit_solution(160086010396666674)
XLA Ops:
  0.6 30.3 %newton_step.1 = (f32[128,128]{1,0:T(8,128)}, f32[128,128]{1,0:T(8,128)}) custom-call(f32[128,128]{1,0:T(8,128)} %bitcast.7, f32[128,128]{1,0:T(8,128)} %bitcast.8, f32[1,128]{1,0:T(1,128)} %initial_hbm.1, f32[128,128]{1,0:T(8,128)} %bitcast.9, f32[128,384]{1,0:T(8,128)} %in_weight_hbm.1, f32[128,384]{1,0:T(8,128)} %weight_hbm.1, f32[384]{0:T(512)} %bias_hbm.1), custom_call_target="tpu_custom_call" | custom-call | tf_op jit(solution)/shard_map/newton_step/pallas_call | solution.py:440
  30.9 0.0 copy-start
  30.9 1.5 %copy.11 = f32[1,128,128]{2,1,0:T(8,128)} copy(f32[1,128,128]{2,1,0:T(8,128)} %bitcast.6) | data formatting | bytes 131072
  32.4 0.0 copy-done
  32.4 0.6 %copy.12 = f32[1,128,128]{2,1,0:T(8,128)} copy(f32[1,128,128]{2,1,0:T(8,128)S(1)} %bitcast.5) | data formatting | bytes 131072
Async XLA Ops:
  30.9 1.5 %copy-start = (f32[128,128]{1,0:T(8,128)S(1)}, f32[128,128]{1,0:T(8,128)}, u32[]{:S(2)}) copy-start(f32[128,128]{1,0:T(8,128)} %get-tuple-element.5) | copy-start | bytes 196612

commit v6 on v5

--- a/solution.py
+++ b/solution.py
@@ -121,6 +121,7 @@
     behind_ref,
     out_ahead_ref,
     out_behind_ref,
+    entry_ref,
     row_sems,
     pair_send,
     pair_recv,
@@ -269,7 +270,6 @@
 
     node = levels[-1][0]
     tall = width + 2 * SENT
-    half = tall // 2
 
     def write_message(target, node):
         target[pl.ds(0, width + SENT), :] = node[0][: width + SENT]
@@ -299,17 +299,6 @@
     sibling_copy = send(pair_ref.at[0, sides[0]], 0, partners[0])
     sibling_copy.wait_recv()
     pairs.append([read_message(pair_ref.at[0, i]) for i in (0, 1)])
-    node = merge(*pairs[0])
-
-    write_message(pair_ref.at[1, sides[1]], node)
-    my_half = pl.ds(pl.multiple_of(half * sides[0], SENT), half)
-    half_copy = send(pair_ref.at[1, sides[1], my_half], 1, partners[1])
-    half_copy.wait_recv()
-    shared_copy = send(pair_ref.at[1, 1 - sides[1], my_half], 2, partners[0])
-    shared_copy.wait_recv()
-    pairs.append([read_message(pair_ref.at[1, i]) for i in (0, 1)])
-    node = merge(*pairs[1])
-    copies = [sibling_copy, half_copy, shared_copy]
 
     ahead_copy = pltpu.make_async_remote_copy(
         src_ref=out_ahead_ref,
@@ -325,59 +314,93 @@
         recv_sem=behind_sems.at[1],
         device_id=at(me - GROUP),
     )
-
-    def doubled(ref):
-        return jnp.concatenate([ref[...], ref[...]], axis=0)
-
-    def pass_forward():
-        @pl.when(group == 0)
+    entry_copy = pltpu.make_async_remote_copy(
+        src_ref=entry_ref,
+        dst_ref=entry_ref,
+        send_sem=pair_send.at[2],
+        recv_sem=pair_recv.at[2],
+        device_id=at(partners[0]),
+    )
+
+    def doubled(rows):
+        return jnp.concatenate([rows, rows], axis=0)
+
+    @pl.when(sides[0] == 1)
+    def _():
+        write_message(pair_ref.at[1, sides[1]], merge(*pairs[0]))
+        plane_copy = send(pair_ref.at[1, sides[1]], 1, partners[1])
+        plane_copy.wait_recv()
+        early, late = [read_message(pair_ref.at[1, i]) for i in (0, 1)]
+        node = merge(early, late)
+
+        def pass_forward():
+            @pl.when(group == 0)
+            def _():
+                ahead_ref[...] = jnp.broadcast_to(initial_ref[...], ahead_ref.shape)
+
+            @pl.when(group > 0)
+            def _():
+                ahead_copy.wait_recv()
+
+            @pl.when(group < groups - 1)
+            def _():
+                out_ahead_ref[...] = go_forward(node, doubled(ahead_ref[...]))[:SENT]
+                ahead_copy.start()
+
+        def pass_back():
+            @pl.when(group == groups - 1)
+            def _():
+                behind_ref[...] = jnp.zeros_like(behind_ref)
+                out_behind_ref[...] = node[2][:SENT]
+
+            @pl.when(group < groups - 1)
+            def _():
+                behind_copy.wait_recv()
+                out_behind_ref[...] = go_back(node, doubled(behind_ref[...]))[:SENT]
+
+            @pl.when(group > 0)
+            def _():
+                behind_copy.start()
+
+        @pl.when(group < groups // 2)
         def _():
-            ahead_ref[...] = jnp.broadcast_to(initial_ref[...], ahead_ref.shape)
+            pass_forward()
+            pass_back()
+
+        @pl.when(group >= groups // 2)
+        def _():
+            pass_back()
+            pass_forward()
+
+        state, costate = doubled(ahead_ref[...]), doubled(behind_ref[...])
+        is_late = sides[1] == 1
+        entry_ref[pl.ds(0, SENT), :] = jnp.where(is_late, go_forward(early, state), state)[:SENT]
+        entry_ref[pl.ds(SENT, SENT), :] = jnp.where(is_late, costate, go_back(late, costate))[
+            :SENT
+        ]
+        entry_copy.start()
+        plane_copy.wait_send()
+
+        @pl.when(group < groups - 1)
+        def _():
+            ahead_copy.wait_send()
 
         @pl.when(group > 0)
         def _():
-            ahead_copy.wait_recv()
-
-        @pl.when(group < groups - 1)
-        def _():
-            out_ahead_ref[...] = go_forward(node, doubled(ahead_ref))[:SENT]
-            ahead_copy.start()
-
-    def pass_back():
-        @pl.when(group == groups - 1)
-        def _():
-            behind_ref[...] = jnp.zeros_like(behind_ref)
-            out_behind_ref[...] = node[2][:SENT]
-
-        @pl.when(group < groups - 1)
-        def _():
-            behind_copy.wait_recv()
-
-            out_behind_ref[...] = go_back(node, doubled(behind_ref))[:SENT]
-
-        @pl.when(group > 0)
-        def _():
-            behind_copy.start()
-
-    @pl.when(group < groups // 2)
-    def _():
-        pass_forward()
-        pass_back()
-
-    @pl.when(group >= groups // 2)
-    def _():
-        pass_back()
-        pass_forward()
-
-    state = doubled(ahead_ref)
-    costate = doubled(behind_ref)
-    for level in reversed(range(len(GROUP_LEVELS))):
-        early, late = pairs[level]
-        is_late = sides[level] == 1
-        state, costate = (
-            jnp.where(is_late, go_forward(early, state), state),
-            jnp.where(is_late, costate, go_back(late, costate)),
-        )
+            behind_copy.wait_send()
+
+    @pl.when(sides[0] == 0)
+    def _():
+        entry_copy.wait_recv()
+
+    state = doubled(entry_ref[pl.ds(0, SENT), :])
+    costate = doubled(entry_ref[pl.ds(SENT, SENT), :])
+    early, late = pairs[0]
+    is_late = sides[0] == 1
+    state, costate = (
+        jnp.where(is_late, go_forward(early, state), state),
+        jnp.where(is_late, costate, go_back(late, costate)),
+    )
 
     entries = [(state, costate)]
     for nodes in reversed(levels[:-1]):
@@ -416,16 +439,11 @@
     def _():
         row_copy.wait_send()
 
-    for copy in copies:
-        copy.wait_send()
-
-    @pl.when(group < groups - 1)
-    def _():
-        ahead_copy.wait_send()
-
-    @pl.when(group > 0)
-    def _():
-        behind_copy.wait_send()
+    sibling_copy.wait_send()
+
+    @pl.when(sides[0] == 1)
+    def _():
+        entry_copy.wait_send()
 
 
 def per_device(
@@ -463,6 +481,7 @@
             vmem((SENT, width)),
             vmem((SENT, width)),
             vmem((SENT, width)),
+            vmem((2 * SENT, width)),
             pair_sems,
             pltpu.SemaphoreType.DMA((3,)),
             pltpu.SemaphoreType.DMA((3,)),

time: 33.2 us -> 31 us (0.934)
  Pallas kernels: 30.3 us -> 28 us
    pallas_call x1, Pallas kernels: 30.3 us -> 28 us  [per_device(): pl.pallas_call(functools.partial(kernel, seq_count), out_shape=(out, out)...]
where the time goes in v6:
time: 31 us; the launch traced here: 30.8 us
  Pallas kernels  28 us (90%)
  local copies, waits for them, and re-layouts  2.14 us (7%)
  between operations  0.65 us (2%)
    pallas_call x1, Pallas kernels, per_device(): pl.pallas_call(functools.partial(kernel, seq_count), out_shape=(out, out)...  28 us
    unnamed x4, local copies, waits for them, and re-layouts  2.14 us

profile of v6, /device:TPU:0, one launch (start us, length us, event | category | flops | bytes accessed | tf_op | source)
XLA Modules:
  0.0 30.8 jit_solution(15670063946557415342)
XLA Ops:
  0.6 28.0 %newton_step.1 = (f32[128,128]{1,0:T(8,128)}, f32[128,128]{1,0:T(8,128)}) custom-call(f32[128,128]{1,0:T(8,128)} %bitcast.7, f32[128,128]{1,0:T(8,128)} %bitcast.8, f32[1,128]{1,0:T(1,128)} %initial_hbm.1, f32[128,128]{1,0:T(8,128)} %bitcast.9, f32[128,384]{1,0:T(8,128)} %in_weight_hbm.1, f32[128,384]{1,0:T(8,128)} %weight_hbm.1, f32[384]{0:T(512)} %bias_hbm.1), custom_call_target="tpu_custom_call" | custom-call | tf_op jit(solution)/shard_map/newton_step/pallas_call | solution.py:458
  28.7 0.0 copy-start
  28.7 1.5 %copy.11 = f32[1,128,128]{2,1,0:T(8,128)} copy(f32[1,128,128]{2,1,0:T(8,128)} %bitcast.6) | data formatting | bytes 131072
  30.2 0.0 copy-done
  30.2 0.6 %copy.12 = f32[1,128,128]{2,1,0:T(8,128)} copy(f32[1,128,128]{2,1,0:T(8,128)S(1)} %bitcast.5) | data formatting | bytes 131072
Async XLA Ops:
  28.7 1.5 %copy-start = (f32[128,128]{1,0:T(8,128)S(1)}, f32[128,128]{1,0:T(8,128)}, u32[]{:S(2)}) copy-start(f32[128,128]{1,0:T(8,128)} %get-tuple-element.5) | copy-start | bytes 196612

commit v7 on v6

--- a/solution.py
+++ b/solution.py
@@ -133,6 +133,9 @@
     me = lax.axis_index("seq")
     groups = seq_count // GROUP
     group = me // GROUP
+    odd, couple = group % 2, group // 2
+    after = groups // 2 - 1 - couple
+    neighbour = me + GROUP - 2 * GROUP * odd
 
     def at(place):
         return {"seq": place}
@@ -153,7 +156,7 @@
 
     barrier = pltpu.get_barrier_semaphore()
     greeted = jnp.int32(0)
-    for distance in (1, GROUP):
+    for distance in (1, GROUP, 2 * GROUP):
 
         @pl.when(me >= distance)
         def _():
@@ -283,14 +286,17 @@
             jnp.concatenate([adjoint, adjoint], axis=0),
         )
 
-    def send(ref, index, partner):
-        copy = pltpu.make_async_remote_copy(
+    def copy_to(ref, index, partner):
+        return pltpu.make_async_remote_copy(
             src_ref=ref,
             dst_ref=ref,
             send_sem=pair_send.at[index],
             recv_sem=pair_recv.at[index],
             device_id=at(partner),
         )
+
+    def send(ref, index, partner):
+        copy = copy_to(ref, index, partner)
         copy.start()
         return copy
 
@@ -300,20 +306,20 @@
     sibling_copy.wait_recv()
     pairs.append([read_message(pair_ref.at[0, i]) for i in (0, 1)])
 
-    ahead_copy = pltpu.make_async_remote_copy(
-        src_ref=out_ahead_ref,
-        dst_ref=ahead_ref,
-        send_sem=ahead_sems.at[0],
-        recv_sem=ahead_sems.at[1],
-        device_id=at(me + GROUP),
-    )
-    behind_copy = pltpu.make_async_remote_copy(
-        src_ref=out_behind_ref,
-        dst_ref=behind_ref,
-        send_sem=behind_sems.at[0],
-        recv_sem=behind_sems.at[1],
-        device_id=at(me - GROUP),
-    )
+    def pass_to(source, target, sems, distance):
+        return [
+            pltpu.make_async_remote_copy(
+                src_ref=source,
+                dst_ref=target,
+                send_sem=sems.at[turn - 1],
+                recv_sem=sems.at[2],
+                device_id=at(me + distance * turn),
+            )
+            for turn in (1, 2)
+        ]
+
+    ahead_copies = pass_to(out_ahead_ref, ahead_ref, ahead_sems, GROUP)
+    behind_copies = pass_to(out_behind_ref, behind_ref, behind_sems, -GROUP)
     entry_copy = pltpu.make_async_remote_copy(
         src_ref=entry_ref,
         dst_ref=entry_ref,
@@ -333,34 +339,66 @@
         early, late = [read_message(pair_ref.at[1, i]) for i in (0, 1)]
         node = merge(early, late)
 
+        write_message(pair_ref.at[2, odd], node)
+        offsets_copy = copy_to(pair_ref.at[2, odd, pl.ds(width, 2 * SENT)], 3, neighbour)
+        matrix_copy = copy_to(pair_ref.at[2, odd, pl.ds(0, width)], 4, neighbour)
+        offsets_copy.start()
+
+        @pl.when(1 - odd + after > 0)
+        def _():
+            matrix_copy.start()
+
         def pass_forward():
-            @pl.when(group == 0)
+            @pl.when(couple == 0)
             def _():
                 ahead_ref[...] = jnp.broadcast_to(initial_ref[...], ahead_ref.shape)
 
-            @pl.when(group > 0)
+            @pl.when(couple > 0)
             def _():
-                ahead_copy.wait_recv()
-
-            @pl.when(group < groups - 1)
+                ahead_copies[0].wait_recv()
+
+            @pl.when(odd == 1)
             def _():
-                out_ahead_ref[...] = go_forward(node, doubled(ahead_ref[...]))[:SENT]
-                ahead_copy.start()
+                offsets_copy.wait_recv()
+                matrix_copy.wait_recv()
+                state = go_forward(read_message(pair_ref.at[2, 0]), doubled(ahead_ref[...]))
+                ahead_ref[...] = state[:SENT]
+
+                @pl.when(after > 0)
+                def _():
+                    out_ahead_ref[...] = go_forward(node, state)[:SENT]
+                    for copy in ahead_copies:
+                        copy.start()
 
         def pass_back():
-            @pl.when(group == groups - 1)
+            @pl.when(after > 0)
+            def _():
+                behind_copies[0].wait_recv()
+
+            @pl.when(after == 0)
             def _():
                 behind_ref[...] = jnp.zeros_like(behind_ref)
-                out_behind_ref[...] = node[2][:SENT]
-
-            @pl.when(group < groups - 1)
+
+            @pl.when(odd == 0)
             def _():
-                behind_copy.wait_recv()
-                out_behind_ref[...] = go_back(node, doubled(behind_ref[...]))[:SENT]
-
-            @pl.when(group > 0)
-            def _():
-                behind_copy.start()
+                offsets_copy.wait_recv()
+
+                @pl.when(after > 0)
+                def _():
+                    matrix_copy.wait_recv()
+                    behind_ref[...] = go_back(
+                        read_message(pair_ref.at[2, 1]), doubled(behind_ref[...])
+                    )[:SENT]
+
+                @pl.when(after == 0)
+                def _():
+                    behind_ref[...] = pair_ref[2, 1, pl.ds(width + SENT, SENT), :]
+
+                @pl.when(couple > 0)
+                def _():
+                    out_behind_ref[...] = go_back(node, doubled(behind_ref[...]))[:SENT]
+                    for copy in behind_copies:
+                        copy.start()
 
         @pl.when(group < groups // 2)
         def _():
@@ -380,14 +418,21 @@
         ]
         entry_copy.start()
         plane_copy.wait_send()
-
-        @pl.when(group < groups - 1)
-        def _():
-            ahead_copy.wait_send()
-
-        @pl.when(group > 0)
-        def _():
-            behind_copy.wait_send()
+        offsets_copy.wait_send()
+
+        @pl.when(1 - odd + after > 0)
+        def _():
+            matrix_copy.wait_send()
+
+        @pl.when(odd * after > 0)
+        def _():
+            for copy in ahead_copies:
+                copy.wait_send()
+
+        @pl.when((1 - odd) * couple > 0)
+        def _():
+            for copy in behind_copies:
+                copy.wait_send()
 
     @pl.when(sides[0] == 0)
     def _():
@@ -475,7 +520,7 @@
             vmem((rows, width)),
             vmem((blocks, tall, width)),
             vmem((blocks, width, width)),
-            vmem((len(GROUP_LEVELS), 2, width + 2 * SENT, width)),
+            vmem((len(GROUP_LEVELS) + 1, 2, width + 2 * SENT, width)),
             vmem((8, width)),
             vmem((SENT, width)),
             vmem((SENT, width)),
@@ -483,10 +528,10 @@
             vmem((SENT, width)),
             vmem((2 * SENT, width)),
             pair_sems,
+            pltpu.SemaphoreType.DMA((5,)),
+            pltpu.SemaphoreType.DMA((5,)),
             pltpu.SemaphoreType.DMA((3,)),
             pltpu.SemaphoreType.DMA((3,)),
-            pair_sems,
-            pair_sems,
         ],
         compiler_params=pltpu.CompilerParams(
             collective_id=0, has_side_effects=True, vmem_limit_bytes=64 * 1024 * 1024

time: 31 us -> 29.7 us (0.958)
  Pallas kernels: 28 us -> 26.8 us
    pallas_call x1, Pallas kernels: 28 us -> 26.8 us  [per_device(): pl.pallas_call(functools.partial(kernel, seq_count), out_shape=(out, out)...]
where the time goes in v7:
time: 29.7 us; the launch traced here: 29.6 us
  Pallas kernels  26.8 us (90%)
  local copies, waits for them, and re-layouts  2.14 us (7%)
  between operations  0.65 us (2%)
    pallas_call x1, Pallas kernels, per_device(): pl.pallas_call(functools.partial(kernel, seq_count), out_shape=(out, out)...  26.8 us
    unnamed x4, local copies, waits for them, and re-layouts  2.14 us

profile of v7, /device:TPU:0, one launch (start us, length us, event | category | flops | bytes accessed | tf_op | source)
XLA Modules:
  0.0 29.6 jit_solution(3570393692426684044)
XLA Ops:
  0.6 26.8 %newton_step.1 = (f32[128,128]{1,0:T(8,128)}, f32[128,128]{1,0:T(8,128)}) custom-call(f32[128,128]{1,0:T(8,128)} %bitcast.7, f32[128,128]{1,0:T(8,128)} %bitcast.8, f32[1,128]{1,0:T(1,128)} %initial_hbm.1, f32[128,128]{1,0:T(8,128)} %bitcast.9, f32[128,384]{1,0:T(8,128)} %in_weight_hbm.1, f32[128,384]{1,0:T(8,128)} %weight_hbm.1, f32[384]{0:T(512)} %bias_hbm.1), custom_call_target="tpu_custom_call" | custom-call | tf_op jit(solution)/shard_map/newton_step/pallas_call | solution.py:503
  27.4 0.0 copy-start
  27.4 1.5 %copy.11 = f32[1,128,128]{2,1,0:T(8,128)} copy(f32[1,128,128]{2,1,0:T(8,128)} %bitcast.6) | data formatting | bytes 131072
  28.9 0.0 copy-done
  28.9 0.6 %copy.12 = f32[1,128,128]{2,1,0:T(8,128)} copy(f32[1,128,128]{2,1,0:T(8,128)S(1)} %bitcast.5) | data formatting | bytes 131072
Async XLA Ops:
  27.4 1.5 %copy-start = (f32[128,128]{1,0:T(8,128)S(1)}, f32[128,128]{1,0:T(8,128)}, u32[]{:S(2)}) copy-start(f32[128,128]{1,0:T(8,128)} %get-tuple-element.5) | copy-start | bytes 196612

commit v8 on v7

--- a/solution.py
+++ b/solution.py
@@ -54,16 +54,6 @@
         preferred_element_type=jnp.float32,
     )
     return out[:count, :width] + out[count:, :width] + out[:count, width:]
-
-
-def row_sums(matrix):
-    ones = jnp.ones((PAD, 2 * matrix.shape[1]), jnp.bfloat16)
-    return lax.dot_general(
-        ones,
-        jnp.concatenate(split(matrix), axis=1),
-        NT,
-        preferred_element_type=jnp.float32,
-    )
 
 
 def node_of(mapped, adjoint):
@@ -114,7 +104,6 @@
     term_ref,
     offset_ref,
     map_ref,
-    acc_ref,
     pair_ref,
     row_ref,
     ahead_ref,
@@ -248,31 +237,59 @@
     for block in range(blocks):
         row = block * BLOCK
         first = coupling(row) + jnp.where(diagonal, keep_ref[pl.ds(row, 1), :], 0.0)
-        map_ref[block, pl.ds(0, width), :] = first
-        map_ref[block, pl.ds(width, PAD), :] = jnp.broadcast_to(
-            offset_ref[pl.ds(row, 1), :], (PAD, width)
+        map_ref[block] = first
+
+    def advance(states, now):
+        mapped = few_rows(states, weight_parts, NN)
+        states = keep_ref[now, :] * states + offset_ref[now, :]
+        for part in range(3):
+            columns = slice(part * width, (part + 1) * width)
+            states = states + term_ref[part, now, :] * mapped[:, columns]
+        return states
+
+    def retreat(costates, now):
+        spread = jnp.concatenate(
+            [term_ref[part, now, :] * costates for part in range(3)], axis=1
         )
-        acc_ref[block] = first * cotan_ref[pl.ds(row, 1), :]
+        return keep_ref[now, :] * costates + few_rows(spread, weight_parts, NT)
+
+    def steps_at(step):
+        return pl.ds(step, blocks, stride=BLOCK)
 
     def gather_step(step, carry):
+        offsets, adjoints = carry
         for block in range(blocks):
             row = block * BLOCK + step
             mapped = map_ref[block]
-            moved = mapped * keep_ref[pl.ds(row, 1), :] + product(mapped, coupling(row))
-            map_ref[block, pl.ds(0, width), :] = moved[:width]
-            map_ref[block, pl.ds(width, PAD), :] = moved[width:] + offset_ref[pl.ds(row, 1), :]
-            acc_ref[block] += moved[:width] * cotan_ref[pl.ds(row, 1), :]
-        return carry
-
-    lax.fori_loop(1, BLOCK, gather_step, 0)
-
-    levels = [[node_of(map_ref[block], row_sums(acc_ref[block])) for block in range(blocks)]]
+            map_ref[block] = mapped * keep_ref[pl.ds(row, 1), :] + product(mapped, coupling(row))
+        back = steps_at(BLOCK - step)
+        return advance(offsets, steps_at(step)), retreat(cotan_ref[back, :] + adjoints, back)
+
+    offsets, adjoints = lax.fori_loop(
+        1,
+        BLOCK,
+        gather_step,
+        (offset_ref[steps_at(0), :], jnp.zeros((blocks, width), jnp.float32)),
+    )
+    adjoints = retreat(cotan_ref[steps_at(0), :] + adjoints, steps_at(0))
+
+    def repeated(rows, block):
+        return jnp.broadcast_to(rows[block : block + 1], (PAD, width))
+
+    levels = [
+        [
+            node_of(
+                jnp.concatenate([map_ref[block], repeated(offsets, block)], axis=0),
+                repeated(adjoints, block),
+            )
+            for block in range(blocks)
+        ]
+    ]
     while len(levels[-1]) > 1:
         nodes = levels[-1]
         levels.append([merge(nodes[i], nodes[i + 1]) for i in range(0, len(nodes), 2)])
 
     node = levels[-1][0]
-    tall = width + 2 * SENT
 
     def write_message(target, node):
         target[pl.ds(0, width + SENT), :] = node[0][: width + SENT]
@@ -461,22 +478,12 @@
 
     def apply_step(step, carry):
         states, costates = carry
-        now = pl.ds(step, blocks, stride=BLOCK)
-        mapped = few_rows(states, weight_parts, NN)
-        states = keep_ref[now, :] * states + offset_ref[now, :]
-        for part in range(3):
-            columns = slice(part * width, (part + 1) * width)
-            states = states + term_ref[part, now, :] * mapped[:, columns]
+        now, back = steps_at(step), steps_at(BLOCK - 1 - step)
+        states = advance(states, now)
         state_out[now, :] = states
-
-        back = pl.ds(BLOCK - 1 - step, blocks, stride=BLOCK)
         costates = cotan_ref[back, :] + costates
         adjoint_out[back, :] = costates
-        spread = jnp.concatenate(
-            [term_ref[part, back, :] * costates for part in range(3)], axis=1
-        )
-        costates = keep_ref[back, :] * costates + few_rows(spread, weight_parts, NT)
-        return states, costates
+        return states, retreat(costates, back)
 
     lax.fori_loop(0, BLOCK, apply_step, (states, costates))
 
@@ -497,7 +504,6 @@
     rows, width = trajectory.shape[1:]
     blocks = rows // BLOCK
     out = jax.ShapeDtypeStruct((rows, width), jnp.float32)
-    tall = width + PAD
     vmem = functools.partial(pltpu.VMEM, dtype=jnp.float32)
     pair_sems = pltpu.SemaphoreType.DMA((2,))
     new_state, adjoint = pl.pallas_call(
@@ -518,7 +524,6 @@
             vmem((rows, width)),
             vmem((3, rows, width)),
             vmem((rows, width)),
-            vmem((blocks, tall, width)),
             vmem((blocks, width, width)),
             vmem((len(GROUP_LEVELS) + 1, 2, width + 2 * SENT, width)),
             vmem((8, width)),

time: 29.7 us -> 29.5 us (level)
  Pallas kernels: 26.8 us -> 26.5 us
where the time goes in v8:
time: 29.5 us; the launch traced here: 29.3 us
  Pallas kernels  26.5 us (90%)
  local copies, waits for them, and re-layouts  2.14 us (7%)
  between operations  0.65 us (2%)
    pallas_call x1, Pallas kernels, per_device(): pl.pallas_call(functools.partial(kernel, seq_count), out_shape=(out, out)...  26.5 us
    unnamed x4, local copies, waits for them, and re-layouts  2.14 us

profile of v8, /device:TPU:0, one launch (start us, length us, event | category | flops | bytes accessed | tf_op | source)
XLA Modules:
  0.0 29.3 jit_solution(16248832571865315284)
XLA Ops:
  0.6 26.5 %newton_step.1 = (f32[128,128]{1,0:T(8,128)}, f32[128,128]{1,0:T(8,128)}) custom-call(f32[128,128]{1,0:T(8,128)} %bitcast.7, f32[128,128]{1,0:T(8,128)} %bitcast.8, f32[1,128]{1,0:T(1,128)} %initial_hbm.1, f32[128,128]{1,0:T(8,128)} %bitcast.9, f32[128,384]{1,0:T(8,128)} %in_weight_hbm.1, f32[128,384]{1,0:T(8,128)} %weight_hbm.1, f32[384]{0:T(512)} %bias_hbm.1), custom_call_target="tpu_custom_call" | custom-call | tf_op jit(solution)/shard_map/newton_step/pallas_call | solution.py:509
  27.2 0.0 copy-start
  27.2 1.5 %copy.11 = f32[1,128,128]{2,1,0:T(8,128)} copy(f32[1,128,128]{2,1,0:T(8,128)} %bitcast.6) | data formatting | bytes 131072
  28.7 0.0 copy-done
  28.7 0.6 %copy.12 = f32[1,128,128]{2,1,0:T(8,128)} copy(f32[1,128,128]{2,1,0:T(8,128)S(1)} %bitcast.5) | data formatting | bytes 131072
Async XLA Ops:
  27.2 1.5 %copy-start = (f32[128,128]{1,0:T(8,128)S(1)}, f32[128,128]{1,0:T(8,128)}, u32[]{:S(2)}) copy-start(f32[128,128]{1,0:T(8,128)} %get-tuple-element.5) | copy-start | bytes 196612

commit v9 on v8

--- a/solution.py
+++ b/solution.py
@@ -270,6 +270,7 @@
         BLOCK,
         gather_step,
         (offset_ref[steps_at(0), :], jnp.zeros((blocks, width), jnp.float32)),
+        unroll=True,
     )
     adjoints = retreat(cotan_ref[steps_at(0), :] + adjoints, steps_at(0))
 

time: 29.5 us -> 28.7 us (0.973)
  Pallas kernels: 26.5 us -> 25.8 us
    pallas_call x1, Pallas kernels: 26.5 us -> 25.8 us  [per_device(): pl.pallas_call(functools.partial(kernel, seq_count), out_shape=(out, out)...]
where the time goes in v9:
time: 28.7 us; the launch traced here: 28.5 us
  Pallas kernels  25.8 us (90%)
  local copies, waits for them, and re-layouts  2.14 us (7%)
  between operations  0.65 us (2%)
    pallas_call x1, Pallas kernels, per_device(): pl.pallas_call(functools.partial(kernel, seq_count), out_shape=(out, out)...  25.8 us
    unnamed x4, local copies, waits for them, and re-layouts  2.14 us

profile of v9, /device:TPU:0, one launch (start us, length us, event | category | flops | bytes accessed | tf_op | source)
XLA Modules:
  0.0 28.5 jit_solution(17147400068885443786)
XLA Ops:
  0.6 25.8 %newton_step.1 = (f32[128,128]{1,0:T(8,128)}, f32[128,128]{1,0:T(8,128)}) custom-call(f32[128,128]{1,0:T(8,128)} %bitcast.7, f32[128,128]{1,0:T(8,128)} %bitcast.8, f32[1,128]{1,0:T(1,128)} %initial_hbm.1, f32[128,128]{1,0:T(8,128)} %bitcast.9, f32[128,384]{1,0:T(8,128)} %in_weight_hbm.1, f32[128,384]{1,0:T(8,128)} %weight_hbm.1, f32[384]{0:T(512)} %bias_hbm.1), custom_call_target="tpu_custom_call" | custom-call | tf_op jit(solution)/shard_map/newton_step/pallas_call | solution.py:510
  26.4 0.0 copy-start
  26.4 1.5 %copy.11 = f32[1,128,128]{2,1,0:T(8,128)} copy(f32[1,128,128]{2,1,0:T(8,128)} %bitcast.6) | data formatting | bytes 131072
  27.9 0.0 copy-done
  27.9 0.6 %copy.12 = f32[1,128,128]{2,1,0:T(8,128)} copy(f32[1,128,128]{2,1,0:T(8,128)S(1)} %bitcast.5) | data formatting | bytes 131072
Async XLA Ops:
  26.4 1.5 %copy-start = (f32[128,128]{1,0:T(8,128)S(1)}, f32[128,128]{1,0:T(8,128)}, u32[]{:S(2)}) copy-start(f32[128,128]{1,0:T(8,128)} %get-tuple-element.5) | copy-start | bytes 196612
